TPU v7x, 128 devices: a whole 4x4x4 slice. The times are simulated.
128 devices in a mesh: section: 2 (over core), dp: 64 (over x, z, y).
Axes of the slice: x: 4, y: 4, z: 4, core: 2. Of those that a mesh axis runs over, the one named last changes fastest.
Arguments:
- inputs: bfloat16 [2, 8192, 1024], P(None, 'dp'), may hold values from -6 to 6
- cotangent: bfloat16 [2, 8192, 1024], P(None, 'dp'), may hold values from -6 to 6
- seq_lengths: int32 [2, 128], P(None, 'dp'), may hold values from 16 to 112, as said below
- norm_gain: bfloat16 [2, 1024], P('section', 'dp'), may hold values from 0.5 to 1.5
- in_weight: bfloat16 [2, 1024, 4384], P('section', 'dp'), may hold values from -0.1875 to 0.1875
- conv_weight: bfloat16 [2, 4, 2304], P('section', None, 'dp'), may hold values from -3 to 3
- conv_bias: bfloat16 [2, 2304], P('section', 'dp'), may hold values from -0.5 to 0.5
- dt_bias: bfloat16 [2, 32], P('section'), may hold values from -6 to -2
- a_log: bfloat16 [2, 32], P('section'), may hold values from 0 to 2.796875
- skip_gain: bfloat16 [2, 32], P('section'), may hold values from 0.5 to 1.5
- gate_gain: bfloat16 [2, 2048], P('section', 'dp'), may hold values from 0.5 to 1.5
- out_weight: bfloat16 [2, 2048, 1024], P('section', 'dp'), may hold values from -0.125 to 0.125
Outputs:
- section_outputs: float32 [2, 2, 8192, 1024], P('section', None, 'dp')
- input_grads: float32 [2, 2, 8192, 1024], P('section', None, 'dp')
- grad_norm_gain: float32 [2, 1024], P('section', 'dp')
- grad_in_weight: float32 [2, 1024, 4384], P('section', 'dp')
- grad_conv_weight: float32 [2, 4, 2304], P('section', None, 'dp')
- grad_conv_bias: float32 [2, 2304], P('section', 'dp')
- grad_dt_bias: float32 [2, 32], P('section')
- grad_a_log: float32 [2, 32], P('section')
- grad_skip_gain: float32 [2, 32], P('section')
- grad_gate_gain: float32 [2, 2048], P('section', 'dp')
- grad_out_weight: float32 [2, 2048, 1024], P('section', 'dp')
Inputs may be any that keep to these rules, and one draw needn't show every extreme that they name: `seq_lengths`: in each block the two lengths are at least 16 and sum to between 64 and 128; in each micro-batch some block is full, with lengths 128 - 16 and 16.
All inputs are finite; a program needn't handle non-finite values.
Results may differ from a plain program's by a relative error of at most 0.012.
Values may be sent and summed in bfloat16 or wider, within the bound.
No kernel may reach another device: no remote copies, remote signals or barrier semaphores. Data moves between devices by JAX's collectives and lax.ppermute only.
A program may use at most 256 MiB of HBM per device.

v0:
```python
import jax
import jax.numpy as jnp
from jax import lax
from jax.sharding import PartitionSpec as P

H = 32
P_SIZE = 64
N = 128
CONV = 4
DI = 2048
CH = 2304


EPS = 1e-05
PRECISE = lax.Precision.HIGHEST


def shifted_2(block, axis, distance):
    devices = range(lax.axis_size(axis))
    route = [(i - distance, i) for i in devices if i - distance in devices]
    return lax.ppermute(block, axis, route)


def segment_layout(lengths, row_count):
    positions = jnp.arange(row_count, dtype=jnp.int32)
    boundary = lengths[0]
    filled = lengths[0] + lengths[1]
    segment = (positions >= boundary).astype(jnp.int32) + (positions >= filled).astype(jnp.int32)
    active = (positions < filled).astype(jnp.float32)
    return (segment, active)


def mixer(zx, conv_kernel, conv_shift, dt_shift, decay_param, skip_param, gate_param, segment):
    row_count = zx.shape[0]
    gate_part = zx[:, :DI]
    conv_in = zx[:, DI : DI + CH]
    dt_raw = zx[:, DI + CH :]
    conv_total = conv_shift[None, :] + conv_kernel[CONV - 1][None, :] * conv_in
    for lag_steps in range(1, CONV):
        shifted = jnp.concatenate(
            [jnp.zeros((lag_steps, conv_in.shape[1]), conv_in.dtype), conv_in[:-lag_steps]], axis=0
        )
        shifted_seg = jnp.concatenate([jnp.full((lag_steps,), -1, jnp.int32), segment[:-lag_steps]])
        matching = (shifted_seg == segment).astype(conv_in.dtype)
        conv_total = (
            conv_total + conv_kernel[CONV - 1 - lag_steps][None, :] * shifted * matching[:, None]
        )
    conv_out = jax.nn.silu(conv_total)
    head_values = conv_out[:, :DI].reshape(row_count, H, P_SIZE)
    b_in = conv_out[:, DI : DI + N]
    c_out = conv_out[:, DI + N :]
    step_size = jax.nn.softplus(dt_raw + dt_shift[None, :])
    decay_rate = -jnp.exp(decay_param)
    decay_log = jnp.cumsum(step_size * decay_rate[None, :], axis=0)
    positions = jnp.arange(row_count)
    allowed = (positions[:, None] >= positions[None, :]) & (segment[:, None] == segment[None, :])
    log_gap = decay_log.T[:, :, None] - decay_log.T[:, None, :]
    decay_mat = jnp.where(allowed[None], jnp.exp(jnp.where(allowed[None], log_gap, 0.0)), 0.0)
    score_mat = jnp.dot(c_out, b_in.T, precision=PRECISE)
    mixing_mat = score_mat[None] * decay_mat * step_size.T[:, None, :]
    mixed_out = jnp.einsum("hij,jhp->ihp", mixing_mat, head_values, precision=PRECISE)
    mixed_out = mixed_out + skip_param[None, :, None] * head_values
    gated_out = mixed_out.reshape(row_count, DI) * jax.nn.silu(gate_part)
    norm_scale = lax.rsqrt(jnp.mean(gated_out * gated_out, axis=1, keepdims=True) + EPS)
    return gated_out * norm_scale * gate_param[None, :]


def rms_norm(activation, gain_vec):
    return (
        activation
        * lax.rsqrt(jnp.mean(activation * activation, axis=1, keepdims=True) + EPS)
        * gain_vec[None, :]
    )


def layer_forward(activation, lengths, weights, head_params):
    w_in, w_out, norm_vec, conv_kernel, conv_shift, gate_param = weights
    normed = rms_norm(activation, norm_vec.astype(jnp.float32))
    zx = jnp.dot(normed.astype(jnp.bfloat16), w_in, preferred_element_type=jnp.float32)
    segment, active = segment_layout(lengths, activation.shape[0])
    normed_gate = mixer(
        zx,
        conv_kernel.astype(jnp.float32),
        conv_shift.astype(jnp.float32),
        head_params[0],
        head_params[1],
        head_params[2],
        gate_param.astype(jnp.float32),
        segment,
    )
    branch = jnp.dot(normed_gate.astype(jnp.bfloat16), w_out, preferred_element_type=jnp.float32)
    return activation + active[:, None] * branch


def layer_backward(activation, grad_out, lengths, weights, head_params):
    w_in, w_out, norm_vec, conv_kernel, conv_shift, gate_param = weights
    normed, norm_pull = jax.vjp(rms_norm, activation, norm_vec.astype(jnp.float32))
    normed_low = normed.astype(jnp.bfloat16)
    zx = jnp.dot(normed_low, w_in, preferred_element_type=jnp.float32)
    segment, active = segment_layout(lengths, activation.shape[0])

    def local_mixer(zx_in, kernel_in, shift_in, dt_in, decay_in, skip_in, gate_in):
        return mixer(zx_in, kernel_in, shift_in, dt_in, decay_in, skip_in, gate_in, segment)

    normed_gate, mixer_pull = jax.vjp(
        local_mixer,
        zx,
        conv_kernel.astype(jnp.float32),
        conv_shift.astype(jnp.float32),
        head_params[0],
        head_params[1],
        head_params[2],
        gate_param.astype(jnp.float32),
    )
    gate_low = normed_gate.astype(jnp.bfloat16)
    grad_branch = (active[:, None] * grad_out).astype(jnp.bfloat16)
    grad_w_out = jnp.einsum("tf,td->fd", gate_low, grad_branch, preferred_element_type=jnp.float32)
    grad_gate = jnp.einsum("td,fd->tf", grad_branch, w_out, preferred_element_type=jnp.float32)
    pulled = mixer_pull(grad_gate)
    grad_zx = pulled[0].astype(jnp.bfloat16)
    grad_w_in = jnp.einsum("td,tf->df", normed_low, grad_zx, preferred_element_type=jnp.float32)
    grad_normed = jnp.einsum("tf,df->td", grad_zx, w_in, preferred_element_type=jnp.float32)
    grad_act, grad_norm_vec = norm_pull(grad_normed)
    weight_terms = (grad_w_in, grad_w_out, grad_norm_vec, pulled[1], pulled[2], pulled[6])
    head_terms = (pulled[3], pulled[4], pulled[5])
    return (grad_out + grad_act, weight_terms, head_terms)


def add_terms(left_terms, right_terms):
    return tuple((left_item + right_item for left_item, right_item in zip(left_terms, right_terms)))


def masked_terms(terms, weight_flag):
    return tuple(
        (jnp.where(weight_flag, term_item, jnp.zeros_like(term_item)) for term_item in terms)
    )


def body(
    inputs,
    cotangent,
    seq_lengths,
    norm_gain,
    in_weight,
    conv_weight,
    conv_bias,
    dt_bias,
    a_log,
    skip_gain,
    gate_gain,
    out_weight,
):
    section_index = lax.axis_index("section")
    micro_count = inputs.shape[0]
    row_count = inputs.shape[1]
    width = inputs.shape[2]
    shards = (in_weight[0], out_weight[0], norm_gain[0], conv_weight[0], conv_bias[0], gate_gain[0])
    gathered = (
        lax.all_gather(shards[0], "dp", axis=0, tiled=True),
        lax.all_gather(shards[1], "dp", axis=0, tiled=True),
        lax.all_gather(shards[2], "dp", axis=0, tiled=True),
        lax.all_gather(shards[3], "dp", axis=1, tiled=True),
        lax.all_gather(shards[4], "dp", axis=0, tiled=True),
        lax.all_gather(shards[5], "dp", axis=0, tiled=True),
    )
    head_params = (
        dt_bias[0].astype(jnp.float32),
        a_log[0].astype(jnp.float32),
        skip_gain[0].astype(jnp.float32),
    )
    kept_inputs = []
    outputs_by_step = []
    received = jnp.zeros((row_count, width), jnp.float32)
    for step_index in range(micro_count + 1):
        own_rows = inputs[min(step_index, micro_count - 1)].astype(jnp.float32)
        current = jnp.where(section_index == 0, own_rows, received)
        micro_pick = jnp.clip(step_index - section_index, 0, micro_count - 1)
        lengths = lax.dynamic_index_in_dim(seq_lengths, micro_pick, 0, keepdims=False)
        result = layer_forward(current, lengths, gathered, head_params)
        outgoing = result.astype(jnp.bfloat16)
        kept_inputs.append(current)
        outputs_by_step.append(jnp.where(section_index == 0, outgoing.astype(jnp.float32), result))
        if step_index < micro_count:
            received = shifted_2(outgoing, "section", 1).astype(jnp.float32)
    section_outputs = jnp.stack(
        [
            jnp.where(
                section_index == 0, outputs_by_step[micro_index], outputs_by_step[micro_index + 1]
            )
            for micro_index in range(micro_count)
        ]
    )
    backward_weights = (
        lax.all_gather(shards[0], "dp", axis=0, tiled=True),
        lax.all_gather(shards[1], "dp", axis=0, tiled=True),
        lax.all_gather(shards[2], "dp", axis=0, tiled=True),
        lax.all_gather(shards[3], "dp", axis=1, tiled=True),
        lax.all_gather(shards[4], "dp", axis=0, tiled=True),
        lax.all_gather(shards[5], "dp", axis=0, tiled=True),
    )
    stacked_inputs = jnp.stack(kept_inputs)
    weight_sums = None
    head_sums = None
    grads_by_step = []
    incoming = jnp.zeros((row_count, width), jnp.float32)
    for step_index in range(micro_count + 1):
        own_grad = cotangent[min(step_index, micro_count - 1)].astype(jnp.float32)
        grad_out = jnp.where(section_index == 1, own_grad, incoming)
        micro_place = step_index - 1 + section_index
        micro_pick = jnp.clip(micro_place, 0, micro_count - 1)
        in_range = (micro_place >= 0) & (micro_place < micro_count)
        current = lax.dynamic_index_in_dim(
            stacked_inputs, micro_pick + section_index, 0, keepdims=False
        )
        lengths = lax.dynamic_index_in_dim(seq_lengths, micro_pick, 0, keepdims=False)
        grad_input, weight_terms, head_terms = layer_backward(
            current, grad_out, lengths, backward_weights, head_params
        )
        weight_terms = masked_terms(weight_terms, in_range)
        head_terms = masked_terms(head_terms, in_range)
        if weight_sums is None:
            weight_sums = weight_terms
            head_sums = head_terms
        else:
            weight_sums = add_terms(weight_sums, weight_terms)
            head_sums = add_terms(head_sums, head_terms)
        outgoing = grad_input.astype(jnp.bfloat16)
        grads_by_step.append(
            jnp.where(section_index == 0, grad_input, outgoing.astype(jnp.float32))
        )
        if step_index < micro_count:
            incoming = shifted_2(outgoing, "section", -1).astype(jnp.float32)
    input_grads = jnp.stack(
        [
            jnp.where(
                section_index == 0, grads_by_step[micro_index + 1], grads_by_step[micro_index]
            )
            for micro_index in range(micro_count)
        ]
    )
    grad_w_in, grad_w_out, grad_norm_vec, grad_kernel, grad_shift, grad_gate_vec = (
        lax.psum_scatter(weight_sums[0], "dp", scatter_dimension=0, tiled=True),
        lax.psum_scatter(weight_sums[1], "dp", scatter_dimension=0, tiled=True),
        lax.psum_scatter(weight_sums[2], "dp", scatter_dimension=0, tiled=True),
        lax.psum_scatter(weight_sums[3], "dp", scatter_dimension=1, tiled=True),
        lax.psum_scatter(weight_sums[4], "dp", scatter_dimension=0, tiled=True),
        lax.psum_scatter(weight_sums[5], "dp", scatter_dimension=0, tiled=True),
    )
    grad_dt, grad_decay, grad_skip = lax.psum((head_sums[0], head_sums[1], head_sums[2]), "dp")
    return (
        section_outputs[None],
        input_grads[None],
        grad_norm_vec[None],
        grad_w_in[None],
        grad_kernel[None],
        grad_shift[None],
        grad_dt[None],
        grad_decay[None],
        grad_skip[None],
        grad_gate_vec[None],
        grad_w_out[None],
    )


def solution(mesh):
    in_specs = (
        P(None, "dp", None),
        P(None, "dp", None),
        P(None, "dp"),
        P("section", "dp"),
        P("section", "dp", None),
        P("section", None, "dp"),
        P("section", "dp"),
        P("section", None),
        P("section", None),
        P("section", None),
        P("section", "dp"),
        P("section", "dp", None),
    )
    out_specs = (
        P("section", None, "dp", None),
        P("section", None, "dp", None),
        P("section", "dp"),
        P("section", "dp", None),
        P("section", None, "dp"),
        P("section", "dp"),
        P("section", None),
        P("section", None),
        P("section", None),
        P("section", "dp"),
        P("section", "dp", None),
    )
    return jax.shard_map(body, mesh=mesh, in_specs=in_specs, out_specs=out_specs, check_vma=False)
```

profile of v0, /device:TPU:0, one launch (start us, length us, event | category | flops | bytes accessed | tf_op | source)
XLA Modules:
  0.0 1589.3 jit_solution(13661031771864343929)
XLA Ops:
  14.6 351.3 %all-reduce.77 = (bf16[1024]{0:T(1024)(128)(2,1)S(1)}, bf16[2304]{0:T(1024)(128)(2,1)S(1)}, bf16[2048]{0:T(1024)(128)(2,1)S(1)}) all-reduce(bf16[1024]{0:T(1024)(128)(2,1)S(1)} %dynamic-update-slice.1, bf16[2304]{0:T(1024)(128)(2,1)S(1)} %dynamic-update-slice, ...), channel_id=4, replica_groups=mesh['section'=2,'dp'=64] {'dp'}, use_global_device_ids=true, to_apply=%add.70 | all-reduce | flops 5376 | bytes 21504
  366.7 175.6 %all-gather.1 = bf16[1,4,2304]{1,0,2:T(2,128)(2,1)S(1)} all-gather(bf16[1,4,36]{1,0,2:T(2,128)(2,1)S(1)} %copy.121), channel_id=3, replica_groups=mesh['section'=2,'dp'=64] {'dp'}, dimensions={2}, use_global_device_ids=true | all-gather | bytes 18720 | tf_op jit(solution)/shard_map/all_gather | solution.py:162
  560.3 1.9 compare_convert_fusion.3
  562.2 1.9 compare_convert_fusion.9
  565.9 48.6 %slice_reduce_fusion.3 = (f32[2304]{0:T(1024)S(1)}, f32[2304]{0:T(1024)S(1)}, f32[2304]{0:T(1024)S(1)}, f32[2304]{0:T(1024)S(1)}) fusion(f32[1,4,2304]{1,0,2:T(1,128)S(1)} %convert_element_type.549), kind=kLoop, calls=%fused_computation.150 | loop fusion | bytes 73728 | tf_op jit(solution)/shard_map/slice | solution.py:38
  614.6 7.3 fusion.16
  624.1 4.3 divide_multiply_fusion.2
  628.8 4.3 fusion.123
  634.7 4.2 fusion.397
  639.0 1.7 collective-permute-start
  641.6 7.3 fusion.14
  650.3 2.9 divide_multiply_fusion.1
  654.8 6.0 fusion.120
  664.8 2.5 collective-permute-start.1
  668.4 7.5 fusion.12
  679.6 3.7 fusion.10
  685.5 3.8 fusion.164
  691.3 4.3 fusion.114
  695.7 1.7 multiply_reduce_fusion.29
  697.4 2.1 multiply_reduce_fusion.20
  699.5 3.7 multiply_reduce_fusion.23
  703.1 5.6 fusion.166
  709.2 3.4 fusion.111
  714.0 3.5 multiply_reduce_fusion.17
  717.5 3.4 multiply_reduce_fusion.16
  724.0 1.7 fusion.372
  725.7 3.7 multiply_reduce_fusion.35
  729.5 4.0 fusion.6
  733.9 3.9 fusion.2
  742.6 4.9 fusion.162
  749.7 3.6 fusion.163
  755.4 4.6 fusion.237
  764.6 5.3 fusion.102
  769.9 3.0 multiply_reduce_fusion.25
  773.0 4.3 fusion.108
  778.2 2.1 multiply_reduce_fusion.19
  780.3 2.4 multiply_reduce_fusion.22
  782.7 5.7 fusion.168
  788.9 4.2 fusion.105
  795.2 2.6 reduce_window_sum.62
  799.3 3.5 multiply_reduce_fusion.13
  802.8 3.4 multiply_reduce_fusion.12
  811.0 3.8 multiply_reduce_fusion.34
  814.9 2.2 select_bitcast_fusion.1
  817.9 1.7 collective-permute-start.3
  819.7 2.3 fusion.238
  822.0 4.2 select_add_fusion.1
  827.0 9.5 fusion.370
  836.5 7.8 fusion.371
  844.3 2.1 multiply_reduce_fusion.18
  846.5 2.8 multiply_reduce_fusion.21
  849.4 6.0 fusion.170
  855.4 1.7 reduce_window_sum.73
  858.0 2.3 broadcast_multiply_fusion.12
  862.6 4.3 fusion.99
  868.5 1.9 multiply_reduce_fusion.8
  876.1 16.4 %select_add_fusion = f32[1024,4384]{1,0:T(8,128)} fusion(f32[1024,4384]{1,0:T(8,128)} %fusion.371, f32[1024,4384]{1,0:T(8,128)} %fusion.370, pred[]{:T(512)S(6)} %and.60, pred[]{:T(512)S(6)} %and.59, pred[]{:T(512)S(6)} %and.58, f32[3,128,1024]{2,1,0:T(8,128)S(1)} %pad_maximum_fusion, s32[]{:T(128)S(6)} %select_n.377, f32[1024]{0:T(1024)S(1)} %convert_element_type.553, ...), kind=kOutput, calls=%fused_computation | convolution fusion | flops 1173762048 | bytes 56644104 | tf_op jit(solution)/shard_map/td,tf->df/dot_general | solution.py:121
  898.8 2.3 slice.456
  901.2 1.8 fusion.282
  914.3 8.5 multiply_reduce_fusion.33
  923.1 343.5 %all-reduce.76 = (f32[1024]{0:T(1024)S(1)}, f32[4,2304]{1,0:T(4,128)S(1)}, f32[2304]{0:T(1024)S(1)}, f32[1,32]{1,0:T(1,128)}, f32[1,32]{1,0:T(1,128)}, /*index=5*/f32[1,32]{1,0:T(1,128)}, f32[2048]{0:T(1024)S(1)}) all-reduce(f32[1024]{0:T(1024)S(1)} %select_add_fusion.5, ...), channel_id=8, replica_groups=mesh['section'=2,'dp'=64] {'dp'}, use_global_device_ids=true, to_apply=%region_42.44.clone | all-reduce | flops 14688 | bytes 117504
  1269.0 6.1 fusion.117
  1275.2 1.7 multiply_reduce_fusion.30
  1281.9 300.4 %reduce-scatter.4.cloned.1.call-done = f32[16,4384]{1,0:T(8,128)} async-done(((f32[1024,4384]{1,0:T(8,128)}), f32[16,4384]{1,0:T(8,128)}) %reduce-scatter.4.cloned.1.call-update) | async-done | bytes 280592 | tf_op jit(solution)/shard_map/reduce_scatter | solution.py:242
  (581 shorter events, 102.2 us)
Async XLA Ops:
  7.2 607.5 %all-gather.9.cloned.1.call-start = ((), (), s32[]{:S(2)}) async-start(), calls=%async_computation.4 | async-start | bytes 9318400 | tf_op jit(solution)/shard_map/all_gather | solution.py:159
  7.9 626.8 %all-gather.11.cloned.1.call-start = ((), (), s32[]{:S(2)}) async-start(), calls=%async_computation.5 | async-start | bytes 4259840 | tf_op jit(solution)/shard_map/all_gather | solution.py:160
  8.7 1273.3 %reduce-scatter.6.cloned.1.call-start = ((), (), s32[]{:S(2)}) async-start(), calls=%async_computation.3 | async-start | bytes 8519680 | tf_op jit(solution)/shard_map/reduce_scatter | solution.py:243
  542.3 21.9 %copy-start.18 = (bf16[2,128,1024]{2,1,0:T(8,128)(2,1)S(1)}, bf16[2,128,1024]{2,1,0:T(8,128)(2,1)}, u32[]{:S(2)}) copy-start(bf16[2,128,1024]{2,1,0:T(8,128)(2,1)} %param.13) | copy-start | bytes 1572868
  542.3 22.0 %copy-start.172 = (bf16[1,32]{1,0:T(2,128)(2,1)S(1)}, bf16[1,32]{1,0:T(2,128)(2,1)}, u32[]{:S(2)}) copy-start(bf16[1,32]{1,0:T(2,128)(2,1)} %param.22) | copy-start | bytes 196
  542.3 22.1 %copy-start.173 = (bf16[1,32]{1,0:T(2,128)(2,1)S(1)}, bf16[1,32]{1,0:T(2,128)(2,1)}, u32[]{:S(2)}) copy-start(bf16[1,32]{1,0:T(2,128)(2,1)} %param.20) | copy-start | bytes 196
  542.3 22.1 %copy-start.169 = (bf16[1,32]{1,0:T(2,128)(2,1)S(1)}, bf16[1,32]{1,0:T(2,128)(2,1)}, u32[]{:S(2)}) copy-start(bf16[1,32]{1,0:T(2,128)(2,1)} %param.21) | copy-start | bytes 196
  556.2 141.2 %copy-start.156 = (f32[128]{0:T(128)}, f32[128]{0:T(128)S(1)}, u32[]{:S(2)}) copy-start(f32[128]{0:T(128)S(1)} %compare_convert_fusion.12) | copy-start | bytes 1540
  557.5 8.3 copy-start.131
  564.1 119.6 %copy-start.146 = (f32[128]{0:T(128)}, f32[128]{0:T(128)S(1)}, u32[]{:S(2)}) copy-start(f32[128]{0:T(128)S(1)} %get-tuple-element.216) | copy-start | bytes 1540
  564.1 119.6 %copy-start.148 = (f32[128]{0:T(128)}, f32[128]{0:T(128)S(1)}, u32[]{:S(2)}) copy-start(f32[128]{0:T(128)S(1)} %get-tuple-element.218) | copy-start | bytes 1540
  564.1 119.6 %copy-start.153 = (f32[128]{0:T(128)}, f32[128]{0:T(128)S(1)}, u32[]{:S(2)}) copy-start(f32[128]{0:T(128)S(1)} %get-tuple-element.217) | copy-start | bytes 1540
  564.3 90.5 %copy-start.174 = (f32[32]{0:T(128)}, f32[32]{0:T(128)S(1)}, u32[]{:S(2)}) copy-start(f32[32]{0:T(128)S(1)} %bitcast_convert_fusion) | copy-start | bytes 388
  564.4 173.4 %copy-start.114 = (f32[32]{0:T(128)}, f32[32]{0:T(128)S(1)}, u32[]{:S(2)}) copy-start(f32[32]{0:T(128)S(1)} %negate_bitcast_fusion) | copy-start | bytes 388
  614.6 135.0 %copy-start.72 = (f32[2304]{0:T(1024)}, f32[2304]{0:T(1024)S(1)}, u32[]{:S(2)}) copy-start(f32[2304]{0:T(1024)S(1)} %get-tuple-element.55) | copy-start | bytes 27652
  614.6 135.0 %copy-start.74 = (f32[2304]{0:T(1024)}, f32[2304]{0:T(1024)S(1)}, u32[]{:S(2)}) copy-start(f32[2304]{0:T(1024)S(1)} %get-tuple-element.58) | copy-start | bytes 27652
  614.6 135.0 %copy-start.76 = (f32[2304]{0:T(1024)}, f32[2304]{0:T(1024)S(1)}, u32[]{:S(2)}) copy-start(f32[2304]{0:T(1024)S(1)} %get-tuple-element.57) | copy-start | bytes 27652
  614.6 135.0 %copy-start.78 = (f32[2304]{0:T(1024)}, f32[2304]{0:T(1024)S(1)}, u32[]{:S(2)}) copy-start(f32[2304]{0:T(1024)S(1)} %get-tuple-element.56) | copy-start | bytes 27652
  639.0 2.4 collective-permute-start
  654.8 7.7 copy-start
  664.8 3.4 collective-permute-start.1
  668.4 11.2 slice-start
  668.4 11.2 slice-start.1
  679.6 80.3 %copy-start.127 = (f32[128]{0:T(128)}, f32[128]{0:T(128)S(1)}, u32[]{:S(2)}) copy-start(f32[128]{0:T(128)S(1)} %fusion.349) | copy-start | bytes 1540
  713.9 9.0 copy-start.83
  714.0 11.7 slice-start.3
  717.5 8.2 slice-start.4
  733.5 16.1 %copy-start.7 = (f32[128,4384]{0,1:T(8,128)}, f32[128,4384]{0,1:T(8,128)S(1)}, u32[]{:S(2)}) copy-start(f32[128,4384]{0,1:T(8,128)S(1)} %fusion.6) | copy-start | bytes 6733828
  733.6 16.0 %copy-start.38 = (f32[125,2304]{0,1:T(8,128)}, f32[125,2304]{0,1:T(8,128)S(1)}, u32[]{:S(2)}) copy-start(f32[125,2304]{0,1:T(8,128)S(1)} %slice.473) | copy-start | bytes 3456004
  733.7 15.9 %copy-start.32 = (f32[126,2304]{0,1:T(8,128)}, f32[126,2304]{0,1:T(8,128)S(1)}, u32[]{:S(2)}) copy-start(f32[126,2304]{0,1:T(8,128)S(1)} %slice.472) | copy-start | bytes 3483652
  733.8 15.8 copy-start.34
  739.0 8.5 copy-start.25
  761.0 17.2 %collective-permute-start.2 = (bf16[128,1024]{1,0:T(8,128)(2,1)}, bf16[128,1024]{1,0:T(8,128)(2,1)S(1)}, u32[]{:S(2)}, u32[]{:S(2)}) collective-permute-start(bf16[128,1024]{1,0:T(8,128)(2,1)} %get-tuple-element.115), channel_id=1, source_target_pairs={{64,0},{65,1},{66,2},{67,3},{68,4},{69,5},{70,6},{71,7},{72,8},{73... | collective-permute-start | bytes 786440 | tf_op jit(solution)/shard_map/ppermute | solution.py:21
  764.5 18.2 %copy-start.121 = (f32[32,128]{1,0:T(8,128)}, f32[32,128]{1,0:T(8,128)S(1)}, u32[]{:S(2)}) copy-start(f32[32,128]{1,0:T(8,128)S(1)} %copy.138) | copy-start | bytes 49156
  764.5 8.4 copy-start.68
  778.2 36.6 %copy-start.58 = (bf16[128,1024]{1,0:T(8,128)(2,1)}, bf16[128,1024]{1,0:T(8,128)(2,1)S(1)}, u32[]{:S(2)}) copy-start(bf16[128,1024]{1,0:T(8,128)(2,1)S(1)} %collective-permute-done.2) | copy-start | bytes 786436
  799.3 11.7 slice-start.6
  802.8 8.2 slice-start.7
  817.9 4.0 collective-permute-start.3
  826.3 10.2 copy-start.46
  826.3 756.1 %reduce-scatter.4.cloned.1.call-start = ((), (), s32[]{:S(2)}) async-start(), calls=%async_computation.2 | async-start | bytes 18636800 | tf_op jit(solution)/shard_map/reduce_scatter | solution.py:242
  827.0 9.5 copy-start.22
  836.4 7.8 copy-start.3
  836.4 7.8 copy-start.17
  860.4 14.7 copy-start.80
  898.8 8.0 copy-start.88
  914.2 8.6 copy-start.116
  914.2 8.6 copy-start.117
  914.2 8.6 copy-start.108
  914.2 8.6 copy-start.109
  914.2 8.7 copy-start.110
  914.2 8.7 copy-start.89
  914.2 8.7 copy-start.93
  914.2 8.7 copy-start.97
  914.2 8.7 copy-start.100
  914.2 8.7 copy-start.101
  914.2 8.7 copy-start.102
  914.3 8.7 copy-start.103
  914.3 8.7 copy-start.104
  914.3 8.7 copy-start.105
  914.3 8.7 copy-start.106
  914.3 8.7 copy-start.107
  914.3 354.7 %copy-start.86 = (f32[128,128]{1,0:T(8,128)S(1)}, f32[128,128]{1,0:T(8,128)}, u32[]{:S(2)}) copy-start(f32[128,128]{1,0:T(8,128)} %fusion.282) | copy-start | bytes 196612
  1269.0 7.9 copy-start.4
  (132 other events, 398.9 us)
Sparse Core Ops, SparseCore 0:
  10.9 84.0 all-gather.8
  97.8 68.3 all-gather.10
  826.4 364.0 reduce-scatter.5
  1193.3 388.9 reduce-scatter.3
where the time goes:
time: 1600 us; the launch traced here: 1590 us
  blocking collectives  870 us (54%)
  waiting for transfers between devices  303 us (19%)
  matrix products  175 us (11%)
  other arithmetic  107 us (7%)
  local copies, waits for them, and re-layouts  98.9 us (6%)
  between operations  28.4 us (2%)
    unnamed x2, blocking collectives  695 us
    reduce_scatter x1, waiting for transfers between devices, body(): lax.psum_scatter(weight_sums[0], 'dp', scatter_dimension=0, tiled=True)  300 us
    all_gather x1, blocking collectives, body(): lax.all_gather(shards[3], 'dp', axis=1, tiled=True)  176 us
    dot_general x12, matrix products, mixer(): jnp.einsum('hij,jhp->ihp', mixing_mat, head_values, precision=PRECISE)  59.4 us
    slice x1, local copies, waits for them, and re-layouts, mixer(): conv_total = conv_shift[None, :] + conv_kernel[CONV - 1][None, :] * conv_in  48.6 us
    dot_general x3, matrix products, layer_backward(): jnp.einsum('td,tf->df', normed_low, grad_zx, preferred_element_type=jnp.f...  33.7 us
  transfers between devices with their start and end apart: 8, of which 3 were waited for; matrix products, arithmetic and copies ran while one was open for 13% of the time, Pallas kernels for 0%

commit v1 on v0

--- a/solution.py
+++ b/solution.py
@@ -133,6 +133,72 @@
 def masked_terms(terms, weight_flag):
     return tuple(
         (jnp.where(weight_flag, term_item, jnp.zeros_like(term_item)) for term_item in terms)
+    )
+
+
+SMALL = 16
+WIDE = 4480
+
+
+def split_small(flat, n):
+    cuts = [0, 1024 // n, 1024 // n + 4 * CH // n, 1024 // n + 5 * CH // n, 1024 // n + 5 * CH // n + DI // n]
+    parts = [flat[:, a:b] for a, b in zip(cuts[:-1], cuts[1:])]
+    conv = parts[1].reshape(n, CONV, CH // n).transpose(1, 0, 2).reshape(CONV, CH)
+    return parts[0].reshape(-1), conv, parts[2].reshape(-1), parts[3].reshape(-1)
+
+
+def join_small(norm, conv, bias, gate, n):
+    conv_rows = conv.reshape(CONV, n, CH // n).transpose(1, 0, 2).reshape(n, -1)
+    return jnp.concatenate([norm.reshape(n, -1), conv_rows, bias.reshape(n, -1), gate.reshape(n, -1)], axis=1)
+
+
+def gather_weights(in_shard, out_shard, norm, conv, bias, gate):
+    rows = in_shard.shape[0]
+    n = lax.axis_size("dp")
+    small = jnp.concatenate([norm, conv.reshape(-1), bias, gate])
+    small = jnp.pad(small, (0, rows * SMALL - small.shape[0])).reshape(rows, SMALL)
+    zeros = jnp.zeros((rows, WIDE - in_shard.shape[1] - SMALL), in_shard.dtype)
+    pack = jnp.concatenate([in_shard, small, zeros, out_shard[:rows], out_shard[rows:]], axis=1)
+    whole = lax.all_gather(pack, "dp", axis=0, tiled=False)
+    proj = in_shard.shape[1]
+    flat = whole[:, :, proj : proj + SMALL].reshape(n, rows * SMALL)
+    norm_all, conv_all, bias_all, gate_all = split_small(flat, n)
+    w_in = whole[:, :, :proj].reshape(n * rows, proj)
+    out_lo = whole[:, :, WIDE : WIDE + 1024]
+    out_hi = whole[:, :, WIDE + 1024 :]
+    w_out = jnp.concatenate([out_lo, out_hi], axis=1).reshape(2 * n * rows, 1024)
+    return (w_in, w_out, norm_all, conv_all, bias_all, gate_all)
+
+
+def high_low(values):
+    high = values.astype(jnp.bfloat16)
+    return high, (values - high.astype(jnp.float32)).astype(jnp.bfloat16)
+
+
+def reduce_grads(weight_sums, head_sums):
+    n = lax.axis_size("dp")
+    w_in, w_out, norm, conv, bias, gate = weight_sums
+    rows, proj = w_in.shape[0] // n, w_in.shape[1]
+    heads = jnp.concatenate(head_sums)
+    small = join_small(norm, conv, bias, gate, n)
+    small = jnp.pad(small, ((0, 0), (0, rows * SMALL - small.shape[1])))
+    heads_each = jnp.broadcast_to(heads[None], (n, heads.shape[0]))
+    heads_each = jnp.pad(heads_each, ((0, 0), (0, rows * SMALL - heads.shape[0])))
+    extra = [item.reshape(n, rows, SMALL) for item in (*high_low(small), *high_low(heads_each))]
+    zeros = jnp.zeros((n, rows, WIDE - proj - 4 * SMALL), jnp.bfloat16)
+    send_in = jnp.concatenate([w_in.astype(jnp.bfloat16).reshape(n, rows, proj), *extra, zeros], axis=2)
+    send_out = w_out.astype(jnp.bfloat16).reshape(n, 2 * rows, 1024)
+    got_out = lax.all_to_all(send_out, "dp", 0, 0)
+    got_in = lax.all_to_all(send_in, "dp", 0, 0)
+    sum_in = jnp.sum(got_in.astype(jnp.float32), axis=0)
+    sum_out = jnp.sum(got_out.astype(jnp.float32), axis=0)
+    own = [sum_in[:, proj + i * SMALL : proj + (i + 1) * SMALL].reshape(-1) for i in range(4)]
+    flat, heads = own[0] + own[1], (own[2] + own[3])[: heads.shape[0]]
+    cuts = [0, 1024 // n, 1024 // n + 4 * CH // n, 1024 // n + 5 * CH // n, 1024 // n + 5 * CH // n + DI // n]
+    parts = [flat[a:b] for a, b in zip(cuts[:-1], cuts[1:])]
+    return (
+        (sum_in[:, :proj], sum_out, parts[0], parts[1].reshape(CONV, -1), parts[2], parts[3]),
+        (heads[:H], heads[H : 2 * H], heads[2 * H :]),
     )
 
 
@@ -155,14 +221,7 @@
     row_count = inputs.shape[1]
     width = inputs.shape[2]
     shards = (in_weight[0], out_weight[0], norm_gain[0], conv_weight[0], conv_bias[0], gate_gain[0])
-    gathered = (
-        lax.all_gather(shards[0], "dp", axis=0, tiled=True),
-        lax.all_gather(shards[1], "dp", axis=0, tiled=True),
-        lax.all_gather(shards[2], "dp", axis=0, tiled=True),
-        lax.all_gather(shards[3], "dp", axis=1, tiled=True),
-        lax.all_gather(shards[4], "dp", axis=0, tiled=True),
-        lax.all_gather(shards[5], "dp", axis=0, tiled=True),
-    )
+    gathered = gather_weights(*shards)
     head_params = (
         dt_bias[0].astype(jnp.float32),
         a_log[0].astype(jnp.float32),
@@ -190,14 +249,7 @@
             for micro_index in range(micro_count)
         ]
     )
-    backward_weights = (
-        lax.all_gather(shards[0], "dp", axis=0, tiled=True),
-        lax.all_gather(shards[1], "dp", axis=0, tiled=True),
-        lax.all_gather(shards[2], "dp", axis=0, tiled=True),
-        lax.all_gather(shards[3], "dp", axis=1, tiled=True),
-        lax.all_gather(shards[4], "dp", axis=0, tiled=True),
-        lax.all_gather(shards[5], "dp", axis=0, tiled=True),
-    )
+    backward_weights = gathered
     stacked_inputs = jnp.stack(kept_inputs)
     weight_sums = None
     head_sums = None
@@ -238,15 +290,11 @@
             for micro_index in range(micro_count)
         ]
     )
-    grad_w_in, grad_w_out, grad_norm_vec, grad_kernel, grad_shift, grad_gate_vec = (
-        lax.psum_scatter(weight_sums[0], "dp", scatter_dimension=0, tiled=True),
-        lax.psum_scatter(weight_sums[1], "dp", scatter_dimension=0, tiled=True),
-        lax.psum_scatter(weight_sums[2], "dp", scatter_dimension=0, tiled=True),
-        lax.psum_scatter(weight_sums[3], "dp", scatter_dimension=1, tiled=True),
-        lax.psum_scatter(weight_sums[4], "dp", scatter_dimension=0, tiled=True),
-        lax.psum_scatter(weight_sums[5], "dp", scatter_dimension=0, tiled=True),
-    )
-    grad_dt, grad_decay, grad_skip = lax.psum((head_sums[0], head_sums[1], head_sums[2]), "dp")
+    (grad_w_in, grad_w_out, grad_norm_vec, grad_kernel, grad_shift, grad_gate_vec), (
+        grad_dt,
+        grad_decay,
+        grad_skip,
+    ) = reduce_grads(weight_sums, head_sums)
     return (
         section_outputs[None],
         input_grads[None],

time: 1600 us -> 674 us (0.42)
  the two profiles are of different devices: /device:TPU:0 before, /device:TPU:103 now
where the time goes in v1:
time: 674 us; the launch traced here: 665 us
  waiting for transfers between devices  186 us (28%)
  matrix products  179 us (27%)
  other arithmetic  138 us (20%)
  local copies, waits for them, and re-layouts  113 us (17%)
  starting transfers between devices  25.7 us (4%)
  between operations  24.5 us (4%)
    all_to_all x1, waiting for transfers between devices, reduce_grads(): got_in = lax.all_to_all(send_in, 'dp', 0, 0)  113 us
    all_gather x1, waiting for transfers between devices, gather_weights(): whole = lax.all_gather(pack, 'dp', axis=0, tiled=False)  70.4 us
    dot_general x12, matrix products, mixer(): jnp.einsum('hij,jhp->ihp', mixing_mat, head_values, precision=PRECISE)  59.6 us
    dot_general x3, matrix products, layer_backward(): jnp.einsum('td,tf->df', normed_low, grad_zx, preferred_element_type=jnp.f...  35 us
    mul x5, other arithmetic, mixer(): conv_out = jax.nn.silu(conv_total)  20.3 us
    reduce_sum x6, other arithmetic, mixer(): conv_kernel[CONV - 1 - lag_steps][None, :] * shifted * matching[:, None]  19.9 us
    dot_general x3, matrix products, layer_forward(): jnp.dot(normed.astype(jnp.bfloat16), w_in, preferred_element_type=jnp.flo...  18.5 us
    dot_general x3, matrix products, layer_backward(): jnp.einsum('tf,df->td', grad_zx, w_in, preferred_element_type=jnp.float32)  16.5 us
  transfers between devices with their start and end apart: 7, of which 4 were waited for; matrix products, arithmetic and copies ran while one was open for 22% of the time, Pallas kernels for 0%

profile of v1, /device:TPU:103, one launch (start us, length us, event | category | flops | bytes accessed | tf_op | source)
XLA Modules:
  0.0 664.8 jit_solution(11114462428413963285)
XLA Ops:
  31.5 2.0 compare_convert_fusion.9
  35.9 70.4 %all-gather.3.cloned.1.call-done = bf16[1024,6528]{1,0:T(8,128)(2,1)} async-done(((bf16[16,6528]{1,0:T(8,128)(2,1)}), bf16[1024,6528]{1,0:T(8,128)(2,1)}) %all-gather.3.cloned.1.call-update) | async-done | bytes 13369360 | tf_op jit(solution)/shard_map/all_gather | solution.py:162
  107.7 5.0 fusion.389
  112.7 7.7 %slice.540 = bf16[64,16,4384]{2,1,0:T(8,128)(2,1)} slice(bf16[64,16,6528]{2,1,0:T(8,128)(2,1)} %bitcast.394), slice={[0:64], [0:16], [0:4384]} | slice | bytes 17956864 | tf_op jit(solution)/shard_map/slice | solution.py:166
  120.6 7.3 %fusion.220 = f32[128,4384]{0,1:T(8,128)S(1)} fusion(bf16[1024,4384]{1,0:T(8,128)(2,1)} %bitcast.365, f32[1024]{0:T(1024)S(1)} %reshape.1171, f32[128]{0:T(128)S(1)} %add_rsqrt_fusion.5, pred[]{:T(512)S(6)} %eq.206, bf16[2,128,1024]{2,1,0:T(8,128)(2,1)S(1)} %copy-done.14), kind=kOutput, calls=%fused_computation.338 | convolution fusion | flops 1149894656 | bytes 11489793 | tf_op jit(solution)/shard_map/dot_general | solution.py:79
  132.2 4.7 divide_multiply_fusion.2
  138.9 6.0 fusion.93
  145.3 2.5 pad_maximum_fusion
  147.8 2.2 fusion.398
  154.4 3.7 fusion.222
  158.4 3.3 divide_multiply_fusion.1
  164.0 6.1 fusion.90
  177.4 7.5 %fusion.223 = f32[128,4384]{0,1:T(8,128)S(1)} fusion(bf16[1024,4384]{1,0:T(8,128)(2,1)} %bitcast.366, bf16[128,1024]{1,0:T(8,128)(2,1)S(1)} %collective-permute-done.1, f32[128]{0:T(128)S(1)} %add_rsqrt_fusion.1, f32[1024]{0:T(1024)S(1)} %reshape.1171, pred[]{:T(512)S(6)} %eq.206, bf16[2,128,1024]{2,1,0:T(8,128)(2,1)S(1)} %copy-done.14), kind=kOutput, calls=%fused_computation.340 | convolution fusion | flops 1150025728 | bytes 11751937 | tf_op jit(solution)/shard_map/dot_general | solution.py:79
  189.7 3.7 fusion.225
  195.5 3.8 fusion.119
  201.4 4.3 fusion.84
  207.4 2.1 multiply_reduce_fusion.23
  209.5 3.7 multiply_reduce_fusion.20
  213.2 5.8 fusion.121
  219.5 3.4 fusion.81
  224.2 3.5 multiply_reduce_fusion.17
  227.8 3.4 multiply_reduce_fusion.16
  235.9 3.7 multiply_reduce_fusion.35
  239.6 4.3 fusion.231
  244.3 3.9 fusion.234
  253.0 4.9 fusion.117
  260.1 3.6 fusion.118
  265.8 4.6 fusion.192
  270.4 8.8 %fusion.236 = f32[1024,4384]{0,1:T(8,128)} fusion(f32[3,128,1024]{2,1,0:T(8,128)S(1)} %pad_maximum_fusion.1, s32[]{:T(128)S(6)} %select_n.382, f32[128]{0:T(128)S(1)} %copy-done.116, f32[1024]{0:T(1024)S(1)} %reshape.1171, f32[128,2048]{0,1:T(8,128)S(1)} %copy-done.38, f32[128,2304]{0,1:T(8,128)S(1)} %get-tuple-element.134, ...), kind=kOutput, calls=%fused_computation.349 | convolution fusion | flops 1151315968 | bytes 20730372 | tf_op jit(solution)/shard_map/td,tf->df/dot_general | solution.py:121
  280.3 2.2 collective-permute-start.2
  284.4 6.0 fusion.72
  290.5 3.0 multiply_reduce_fusion.25
  293.5 4.3 fusion.78
  297.8 2.5 multiply_reduce_fusion.27
  309.4 4.4 multiply_reduce_fusion.22
  313.8 3.7 multiply_reduce_fusion.19
  317.5 5.8 fusion.123
  324.4 3.5 fusion.75
  329.9 2.6 reduce_window_sum.62
  334.0 3.5 multiply_reduce_fusion.13
  337.6 2.8 multiply_reduce_fusion.12
  345.1 4.5 multiply_reduce_fusion.34
  349.6 8.9 %fusion.237 = f32[1024,4384]{0,1:T(8,128)} fusion(f32[3,128,1024]{2,1,0:T(8,128)S(1)} %pad_maximum_fusion.1, s32[]{:T(128)S(6)} %select_n.388, f32[128]{0:T(128)S(1)} %copy-done.114, f32[1024]{0:T(1024)S(1)} %reshape.1171, f32[128,2048]{0,1:T(8,128)S(1)} %copy-done.36, f32[128,2304]{0,1:T(8,128)S(1)} %get-tuple-element.135, ...), kind=kOutput, calls=%fused_computation.350 | convolution fusion | flops 1151315968 | bytes 20730372 | tf_op jit(solution)/shard_map/td,tf->df/dot_general | solution.py:121
  363.1 2.2 select_bitcast_fusion.1
  368.0 5.5 fusion.193
  373.6 2.1 multiply_reduce_fusion.21
  375.7 2.8 multiply_reduce_fusion.18
  378.6 5.7 fusion.125
  385.4 3.4 fusion.69
  394.3 2.6 reduce_window_sum.73
  398.4 3.5 multiply_reduce_fusion.9
  402.0 3.1 multiply_reduce_fusion.8
  410.2 5.9 add_convert_fusion.1
  416.1 8.7 %all-to-all-start.1 = ((bf16[64,32,1024]{2,1,0:T(8,128)(2,1)}), bf16[64,32,1024]{2,1,0:T(8,128)(2,1)}, u32[]{:S(2)}, u32[]{:S(2)}) async-start(bf16[64,32,1024]{2,1,0:T(8,128)(2,1)} %bitcast.391), calls=%async_computation.1 | async-start | bytes 8388608 | tf_op jit(solution)/shard_map/all_to_all | solution.py:191
  432.0 4.5 multiply_reduce_fusion.6
  438.0 8.3 %multiply_reduce_fusion.33 = (f32[1024]{0:T(1024)S(1)}, f32[128]{0:T(128)}, f32[128,1024]{1,0:T(8,128)}) fusion(f32[3,128,1024]{2,1,0:T(8,128)S(1)} %pad_maximum_fusion.1, s32[]{:T(128)S(6)} %select_n.397, f32[128]{0:T(128)} %copy-done.117, f32[1024]{0:T(1024)S(1)} %reshape.1171, bf16[1024,4384]{1,0:T(8,128)(2,1)} %bitcast.367, ...), kind=kOutput, calls=%fused_computation.294 | convolution fusion | flops 1151708032 | bytes 12280836 | tf_op jit(solution)/shard_map/tf,df->td/dot_general | solution.py:122
  458.8 17.3 %add_convert_fusion = bf16[1024,4384]{0,1:T(8,128)(2,1)} fusion(f32[1024,4384]{0,1:T(8,128)} %fusion.237, f32[1024,4384]{0,1:T(8,128)} %fusion.236, pred[]{:T(512)S(6)} %and.60, pred[]{:T(512)S(6)} %and.59, pred[]{:T(512)S(6)} %and.58, f32[3,128,1024]{2,1,0:T(8,128)S(1)} %pad_maximum_fusion.1, s32[]{:T(128)S(6)} %select_n.397, f32[128]{0:T(128)S(1)} %copy-done.118, ...), kind=kOutput, calls=%fused_computation.1 | convolution fusion | flops 1178251264 | bytes 47665672 | tf_op jit(solution)/shard_map/td,tf->df/dot_general | solution.py:121
  476.1 11.9 %copy.181 = bf16[1024,4384]{1,0:T(8,128)(2,1)} copy(bf16[1024,4384]{0,1:T(8,128)(2,1)} %add_convert_fusion) | data formatting | bytes 17956864 | tf_op jit(solution)/shard_map/convert_element_type | solution.py:189
  488.8 15.5 %concatenate.191 = bf16[64,16,4480]{2,1,0:T(8,128)(2,1)} concatenate(bf16[64,16,4384]{2,1,0:T(8,128)(2,1)} %bitcast.390, bf16[64,16,16]{2,1,0:T(8,128)(2,1)S(1)} %copy-done.59, bf16[64,16,16]{2,1,0:T(8,128)(2,1)S(1)} %copy-done.60, bf16[64,16,16]{2,1,0:T(8,128)(2,1)S(1)} %pad.208, bf16[64,16,16]{2,1,0:T(8,128)(2,1)S(1)} %pad.209, bf16[64,16,32]{2,1,0:T(8,128)(2,1)} %broadcast_in_dim.127), dimensions={2} | concatenate | bytes 18350080 | tf_op jit(solution)/shard_map/concatenate | solution.py:189
  504.3 10.4 %all-to-all-start = ((bf16[64,16,4480]{2,1,0:T(8,128)(2,1)}), bf16[64,16,4480]{2,1,0:T(8,128)(2,1)}, u32[]{:S(2)}, u32[]{:S(2)}) async-start(bf16[64,16,4480]{2,1,0:T(8,128)(2,1)} %concatenate.191), calls=%async_computation | async-start | bytes 18350080 | tf_op jit(solution)/shard_map/all_to_all | solution.py:192
  518.8 5.3 fusion.87
  530.9 3.7 convert_reduce_fusion.1
  534.6 112.9 %all-to-all-done = bf16[64,16,4480]{2,1,0:T(8,128)(2,1)} async-done(((bf16[64,16,4480]{2,1,0:T(8,128)(2,1)}), bf16[64,16,4480]{2,1,0:T(8,128)(2,1)}, u32[]{:S(2)}, u32[]{:S(2)}) %all-to-all-start) | async-done | bytes 9175072 | tf_op jit(solution)/shard_map/all_to_all | solution.py:192
  647.5 5.1 convert_reduce_fusion
  (609 shorter events, 146.6 us)
Async XLA Ops:
  7.2 26.3 %copy-start.14 = (bf16[2,128,1024]{2,1,0:T(8,128)(2,1)S(1)}, bf16[2,128,1024]{2,1,0:T(8,128)(2,1)}, u32[]{:S(2)}) copy-start(bf16[2,128,1024]{2,1,0:T(8,128)(2,1)} %param.13) | copy-start | bytes 1572868
  7.2 26.4 %copy-start.160 = (bf16[1,32]{1,0:T(2,128)(2,1)S(1)}, bf16[1,32]{1,0:T(2,128)(2,1)}, u32[]{:S(2)}) copy-start(bf16[1,32]{1,0:T(2,128)(2,1)} %param.22) | copy-start | bytes 196
  7.2 26.4 %copy-start.161 = (bf16[1,32]{1,0:T(2,128)(2,1)S(1)}, bf16[1,32]{1,0:T(2,128)(2,1)}, u32[]{:S(2)}) copy-start(bf16[1,32]{1,0:T(2,128)(2,1)} %param.20) | copy-start | bytes 196
  7.2 26.5 %copy-start.154 = (bf16[1,32]{1,0:T(2,128)(2,1)S(1)}, bf16[1,32]{1,0:T(2,128)(2,1)}, u32[]{:S(2)}) copy-start(bf16[1,32]{1,0:T(2,128)(2,1)} %param.21) | copy-start | bytes 196
  7.2 99.1 %all-gather.3.cloned.1.call-start = ((), (), s32[]{:S(2)}) async-start(), calls=%async_computation.2 | async-start | bytes 13578240 | tf_op jit(solution)/shard_map/all_gather | solution.py:162
  26.8 8.3 %copy-start.111 = (s32[128]{0:T(128)}, s32[128]{0:T(128)S(1)}, u32[]{:S(2)}) copy-start(s32[128]{0:T(128)S(1)} %fusion.344) | copy-start | bytes 1540
  33.7 105.2 %copy-start.162 = (f32[32]{0:T(128)}, f32[32]{0:T(128)S(1)}, u32[]{:S(2)}) copy-start(f32[32]{0:T(128)S(1)} %bitcast_convert_fusion) | copy-start | bytes 388
  33.7 159.7 %copy-start.92 = (f32[32]{0:T(128)}, f32[32]{0:T(128)S(1)}, u32[]{:S(2)}) copy-start(f32[32]{0:T(128)S(1)} %negate_bitcast_fusion) | copy-start | bytes 388
  138.9 15.5 %slice-start = ((s8[9175040]{0:T(1024)(128)(4,1)}), s8[4194304]{0:T(1024)(128)(4,1)S(1)}, s32[]{:S(2)}) async-start(s8[9175040]{0:T(1024)(128)(4,1)} %bitcast.368), calls=%async_computation.3 | async-start | bytes 8388608
  144.9 9.4 %slice-start.1 = ((s8[9175040]{0:T(1024)(128)(4,1)}), s8[4194304]{0:T(1024)(128)(4,1)S(1)}, s32[]{:S(2)}) async-start(s8[9175040]{0:T(1024)(128)(4,1)} %bitcast.368), calls=%async_computation.4 | async-start | bytes 8388608
  145.3 9.0 %slice-start.2 = ((s8[9175040]{0:T(1024)(128)(4,1)}), s8[786432]{0:T(1024)(128)(4,1)S(1)}, s32[]{:S(2)}) async-start(s8[9175040]{0:T(1024)(128)(4,1)} %bitcast.368), calls=%async_computation.5 | async-start | bytes 1572864
  150.0 3.4 collective-permute-start
  173.7 3.4 collective-permute-start.1
  177.2 7.7 %copy-start.52 = (bf16[128,1024]{1,0:T(8,128)(2,1)}, bf16[128,1024]{1,0:T(8,128)(2,1)S(1)}, u32[]{:S(2)}) copy-start(bf16[128,1024]{1,0:T(8,128)(2,1)S(1)} %collective-permute-done.1) | copy-start | bytes 786436
  177.3 12.3 %slice-start.3 = ((s8[9175040]{0:T(1024)(128)(4,1)}), s8[4194304]{0:T(1024)(128)(4,1)S(1)}, s32[]{:S(2)}) async-start(s8[9175040]{0:T(1024)(128)(4,1)} %bitcast.371), calls=%async_computation.6 | async-start | bytes 8388608
  177.3 12.3 %slice-start.4 = ((s8[9175040]{0:T(1024)(128)(4,1)}), s8[4194304]{0:T(1024)(128)(4,1)S(1)}, s32[]{:S(2)}) async-start(s8[9175040]{0:T(1024)(128)(4,1)} %bitcast.371), calls=%async_computation.7 | async-start | bytes 8388608
  224.2 11.6 %slice-start.6 = ((s8[9175040]{0:T(1024)(128)(4,1)}), s8[4194304]{0:T(1024)(128)(4,1)S(1)}, s32[]{:S(2)}) async-start(s8[9175040]{0:T(1024)(128)(4,1)} %bitcast.374), calls=%async_computation.9 | async-start | bytes 8388608
  227.8 8.1 %slice-start.7 = ((s8[9175040]{0:T(1024)(128)(4,1)}), s8[4194304]{0:T(1024)(128)(4,1)S(1)}, s32[]{:S(2)}) async-start(s8[9175040]{0:T(1024)(128)(4,1)} %bitcast.374), calls=%async_computation.10 | async-start | bytes 8388608
  244.0 16.0 %copy-start.7 = (f32[128,4384]{0,1:T(8,128)}, f32[128,4384]{0,1:T(8,128)S(1)}, u32[]{:S(2)}) copy-start(f32[128,4384]{0,1:T(8,128)S(1)} %fusion.231) | copy-start | bytes 6733828
  244.1 15.9 %copy-start.30 = (f32[125,2304]{0,1:T(8,128)}, f32[125,2304]{0,1:T(8,128)S(1)}, u32[]{:S(2)}) copy-start(f32[125,2304]{0,1:T(8,128)S(1)} %slice.586) | copy-start | bytes 3456004
  244.2 15.8 %copy-start.23 = (f32[126,2304]{0,1:T(8,128)}, f32[126,2304]{0,1:T(8,128)S(1)}, u32[]{:S(2)}) copy-start(f32[126,2304]{0,1:T(8,128)S(1)} %slice.585) | copy-start | bytes 3483652
  244.3 15.8 %copy-start.25 = (f32[127,2304]{0,1:T(8,128)}, f32[127,2304]{0,1:T(8,128)S(1)}, u32[]{:S(2)}) copy-start(f32[127,2304]{0,1:T(8,128)S(1)} %slice.584) | copy-start | bytes 3511300
  249.4 8.5 %copy-start.19 = (f32[127,2304]{0,1:T(8,128)}, f32[127,2304]{0,1:T(8,128)S(1)}, u32[]{:S(2)}) copy-start(f32[127,2304]{0,1:T(8,128)S(1)} %slice.593) | copy-start | bytes 3511300
  270.4 8.8 %copy-start.156 = (f32[128]{0:T(128)S(1)}, f32[128]{0:T(128)}, u32[]{:S(2)}) copy-start(f32[128]{0:T(128)} %copy-done.155) | copy-start | bytes 1540
  280.3 29.1 %collective-permute-start.2 = (bf16[128,1024]{1,0:T(8,128)(2,1)}, bf16[128,1024]{1,0:T(8,128)(2,1)S(1)}, u32[]{:S(2)}, u32[]{:S(2)}) collective-permute-start(bf16[128,1024]{1,0:T(8,128)(2,1)} %get-tuple-element.103), channel_id=1, source_target_pairs={{64,0},{65,1},{66,2},{67,3},{68,4},{69,5},{70,6},{71,7},{72,8},{73... | collective-permute-start | bytes 786440 | tf_op jit(solution)/shard_map/ppermute | solution.py:21
  293.4 6.9 %copy-start.157 = (f32[128]{0:T(128)}, f32[128]{0:T(128)S(1)}, u32[]{:S(2)}) copy-start(f32[128]{0:T(128)S(1)} %get-tuple-element.95) | copy-start | bytes 1540
  309.4 53.7 %copy-start.51 = (bf16[128,1024]{1,0:T(8,128)(2,1)}, bf16[128,1024]{1,0:T(8,128)(2,1)S(1)}, u32[]{:S(2)}) copy-start(bf16[128,1024]{1,0:T(8,128)(2,1)S(1)} %collective-permute-done.2) | copy-start | bytes 786436
  317.5 6.9 %copy-start.73 = (f32[128,128]{1,0:T(8,128)S(1)}, f32[128,128]{1,0:T(8,128)}, u32[]{:S(2)}) copy-start(f32[128,128]{1,0:T(8,128)} %fusion.296) | copy-start | bytes 196612
  317.5 6.9 %copy-start.165 = (f32[32]{0:T(128)S(1)}, f32[32]{0:T(128)}, u32[]{:S(2)}) copy-start(f32[32]{0:T(128)} %copy-done.162) | copy-start | bytes 388
  334.0 11.1 %slice-start.9 = ((s8[9175040]{0:T(1024)(128)(4,1)}), s8[4194304]{0:T(1024)(128)(4,1)S(1)}, s32[]{:S(2)}) async-start(s8[9175040]{0:T(1024)(128)(4,1)} %bitcast.379), calls=%async_computation.12 | async-start | bytes 8388608
  337.6 7.5 %slice-start.10 = ((s8[9175040]{0:T(1024)(128)(4,1)}), s8[4194304]{0:T(1024)(128)(4,1)S(1)}, s32[]{:S(2)}) async-start(s8[9175040]{0:T(1024)(128)(4,1)} %bitcast.379), calls=%async_computation.13 | async-start | bytes 8388608
  349.6 10.4 %copy-start.81 = (f32[2304]{0:T(1024)S(1)}, f32[2304]{0:T(1024)}, u32[]{:S(2)}) copy-start(f32[2304]{0:T(1024)} %get-tuple-element.79) | copy-start | bytes 27652
  366.1 7.4 %copy-start.3 = (bf16[64,32,1024]{2,1,0:T(8,128)(2,1)S(1)}, bf16[64,32,1024]{2,1,0:T(8,128)(2,1)}, u32[]{:S(2)}) copy-start(bf16[64,32,1024]{2,1,0:T(8,128)(2,1)} %copy-done) | copy-start | bytes 12582916
  366.1 7.4 %copy-start.12 = (f32[128,2048]{0,1:T(8,128)S(1)}, f32[128,2048]{0,1:T(8,128)}, u32[]{:S(2)}) copy-start(f32[128,2048]{0,1:T(8,128)} %get-tuple-element.96) | copy-start | bytes 3145732
  366.1 7.4 %copy-start.124 = (f32[128]{0:T(128)S(1)}, f32[128]{0:T(128)}, u32[]{:S(2)}) copy-start(f32[128]{0:T(128)} %fusion.353) | copy-start | bytes 1540
  366.2 7.4 %copy-start.144 = (f32[128]{0:T(128)S(1)}, f32[128]{0:T(128)}, u32[]{:S(2)}) copy-start(f32[128]{0:T(128)} %compare_convert_fusion) | copy-start | bytes 1540
  366.2 7.4 %collective-permute-start.3 = (bf16[128,1024]{1,0:T(8,128)(2,1)S(1)}, bf16[128,1024]{1,0:T(8,128)(2,1)S(1)}, u32[]{:S(2)}, u32[]{:S(2)}) collective-permute-start(bf16[128,1024]{1,0:T(8,128)(2,1)S(1)} %convert_element_type.632), channel_id=1, source_target_pairs={{64,0},{65,1},{66,2},{67,3},{68,4},{69,5},{70,6},{71,7},{72,8},{73... | collective-permute-start | bytes 786440 | tf_op jit(solution)/shard_map/ppermute | solution.py:21
  398.4 11.8 %slice-start.12 = ((s8[8388608]{0:T(1024)(128)(4,1)}), s8[4194304]{0:T(1024)(128)(4,1)S(1)}, s32[]{:S(2)}) async-start(s8[8388608]{0:T(1024)(128)(4,1)} %bitcast.388), calls=%async_computation.15 | async-start | bytes 8388608
  401.9 8.2 %slice-start.13 = ((s8[8388608]{0:T(1024)(128)(4,1)}), s8[4194304]{0:T(1024)(128)(4,1)S(1)}, s32[]{:S(2)}) async-start(s8[8388608]{0:T(1024)(128)(4,1)} %bitcast.388), calls=%async_computation.16 | async-start | bytes 8388608
  416.1 8.7 %copy-start.69 = (f32[128,32]{0,1:T(8,128)S(1)}, f32[128,32]{0,1:T(8,128)}, u32[]{:S(2)}) copy-start(f32[128,32]{0,1:T(8,128)} %copy.174) | copy-start | bytes 49156
  416.1 8.7 %copy-start.75 = (f32[128,32]{0,1:T(8,128)S(1)}, f32[128,32]{0,1:T(8,128)}, u32[]{:S(2)}) copy-start(f32[128,32]{0,1:T(8,128)} %copy.180) | copy-start | bytes 49156
  416.1 10.4 %copy-start.90 = (f32[2048]{0:T(1024)S(1)}, f32[2048]{0:T(1024)}, u32[]{:S(2)}) copy-start(f32[2048]{0:T(1024)} %get-tuple-element.41) | copy-start | bytes 24580
  416.1 10.4 %copy-start.91 = (f32[2048]{0:T(1024)S(1)}, f32[2048]{0:T(1024)}, u32[]{:S(2)}) copy-start(f32[2048]{0:T(1024)} %get-tuple-element.43) | copy-start | bytes 24580
  416.1 14.0 %copy-start.80 = (f32[2304]{0:T(1024)S(1)}, f32[2304]{0:T(1024)}, u32[]{:S(2)}) copy-start(f32[2304]{0:T(1024)} %get-tuple-element.86) | copy-start | bytes 27652
  416.1 88.2 %all-to-all-start.1 = ((bf16[64,32,1024]{2,1,0:T(8,128)(2,1)}), bf16[64,32,1024]{2,1,0:T(8,128)(2,1)}, u32[]{:S(2)}, u32[]{:S(2)}) async-start(bf16[64,32,1024]{2,1,0:T(8,128)(2,1)} %bitcast.391), calls=%async_computation.1 | async-start | bytes 8388608 | tf_op jit(solution)/shard_map/all_to_all | solution.py:191
  426.5 11.4 %copy-start.66 = (f32[128,32]{0,1:T(8,128)}, f32[128,32]{0,1:T(8,128)S(1)}, u32[]{:S(2)}) copy-start(f32[128,32]{0,1:T(8,128)S(1)} %get-tuple-element.162) | copy-start | bytes 49156
  437.9 8.4 %copy-start.96 = (f32[1024]{0:T(1024)S(1)}, f32[1024]{0:T(1024)}, u32[]{:S(2)}) copy-start(f32[1024]{0:T(1024)} %get-tuple-element.35) | copy-start | bytes 12292
  437.9 8.4 %copy-start.97 = (f32[1024]{0:T(1024)S(1)}, f32[1024]{0:T(1024)}, u32[]{:S(2)}) copy-start(f32[1024]{0:T(1024)} %get-tuple-element.37) | copy-start | bytes 12292
  437.9 10.4 %copy-start.82 = (f32[1,2304]{1,0:T(1,128)S(1)}, f32[1,2304]{1,0:T(1,128)}, u32[]{:S(2)}) copy-start(f32[1,2304]{1,0:T(1,128)} %reshape.1153) | copy-start | bytes 27652
  437.9 10.4 %copy-start.83 = (f32[1,2304]{1,0:T(1,128)S(1)}, f32[1,2304]{1,0:T(1,128)}, u32[]{:S(2)}) copy-start(f32[1,2304]{1,0:T(1,128)} %reshape.1154) | copy-start | bytes 27652
  437.9 10.4 %copy-start.84 = (f32[1,2304]{1,0:T(1,128)S(1)}, f32[1,2304]{1,0:T(1,128)}, u32[]{:S(2)}) copy-start(f32[1,2304]{1,0:T(1,128)} %reshape.1155) | copy-start | bytes 27652
  437.9 10.4 %copy-start.85 = (f32[1,2304]{1,0:T(1,128)S(1)}, f32[1,2304]{1,0:T(1,128)}, u32[]{:S(2)}) copy-start(f32[1,2304]{1,0:T(1,128)} %reshape.1156) | copy-start | bytes 27652
  437.9 10.4 %copy-start.86 = (f32[1,2304]{1,0:T(1,128)S(1)}, f32[1,2304]{1,0:T(1,128)}, u32[]{:S(2)}) copy-start(f32[1,2304]{1,0:T(1,128)} %reshape.1157) | copy-start | bytes 27652
  437.9 10.4 %copy-start.87 = (f32[1,2304]{1,0:T(1,128)S(1)}, f32[1,2304]{1,0:T(1,128)}, u32[]{:S(2)}) copy-start(f32[1,2304]{1,0:T(1,128)} %reshape.1158) | copy-start | bytes 27652
  437.9 10.4 %copy-start.88 = (f32[1,2304]{1,0:T(1,128)S(1)}, f32[1,2304]{1,0:T(1,128)}, u32[]{:S(2)}) copy-start(f32[1,2304]{1,0:T(1,128)} %reshape.1159) | copy-start | bytes 27652
  437.9 10.4 %copy-start.89 = (f32[1,2304]{1,0:T(1,128)S(1)}, f32[1,2304]{1,0:T(1,128)}, u32[]{:S(2)}) copy-start(f32[1,2304]{1,0:T(1,128)} %reshape.1160) | copy-start | bytes 27652
  451.5 7.2 %copy-start.67 = (f32[128,32]{0,1:T(8,128)S(1)}, f32[128,32]{0,1:T(8,128)}, u32[]{:S(2)}) copy-start(f32[128,32]{0,1:T(8,128)} %copy-done.66) | copy-start | bytes 49156
  451.5 7.2 %copy-start.118 = (f32[128]{0:T(128)S(1)}, f32[128]{0:T(128)}, u32[]{:S(2)}) copy-start(f32[128]{0:T(128)} %copy-done.117) | copy-start | bytes 1540
  476.0 11.9 %copy-start.95 = (bf16[16,16]{1,0:T(8,128)(2,1)S(1)}, bf16[16,16]{1,0:T(8,128)(2,1)}, u32[]{:S(2)}) copy-start(bf16[16,16]{1,0:T(8,128)(2,1)} %pad.207) | copy-start | bytes 1540
  476.1 12.7 %copy-start.59 = (bf16[64,16,16]{2,1,0:T(8,128)(2,1)S(1)}, bf16[64,16,16]{2,1,0:T(8,128)(2,1)}, u32[]{:S(2)}) copy-start(bf16[64,16,16]{2,1,0:T(8,128)(2,1)} %copy.192) | copy-start | bytes 98308
  476.1 12.7 %copy-start.60 = (bf16[64,16,16]{2,1,0:T(8,128)(2,1)S(1)}, bf16[64,16,16]{2,1,0:T(8,128)(2,1)}, u32[]{:S(2)}) copy-start(bf16[64,16,16]{2,1,0:T(8,128)(2,1)} %copy.193) | copy-start | bytes 98308
  504.3 10.4 %copy-start.112 = (s32[128]{0:T(128)S(1)}, s32[128]{0:T(128)}, u32[]{:S(2)}) copy-start(s32[128]{0:T(128)} %copy-done.111) | copy-start | bytes 1540
  504.3 143.2 %all-to-all-start = ((bf16[64,16,4480]{2,1,0:T(8,128)(2,1)}), bf16[64,16,4480]{2,1,0:T(8,128)(2,1)}, u32[]{:S(2)}, u32[]{:S(2)}) async-start(bf16[64,16,4480]{2,1,0:T(8,128)(2,1)} %concatenate.191), calls=%async_computation | async-start | bytes 18350080 | tf_op jit(solution)/shard_map/all_to_all | solution.py:192
  518.8 7.1 %copy-start.4 = (bf16[64,32,1024]{2,1,0:T(8,128)(2,1)S(1)}, bf16[64,32,1024]{2,1,0:T(8,128)(2,1)}, u32[]{:S(2)}) copy-start(bf16[64,32,1024]{2,1,0:T(8,128)(2,1)} %copy-done) | copy-start | bytes 12582916
  (124 other events, 346.9 us)
Sparse Core Ops, SparseCore 0:
  11.5 94.7 all-gather.2

commit v2 on v0

v2 whole, which is shorter than its diff:
```python
import functools

import jax
import jax.numpy as jnp
from jax import lax
from jax.experimental import pallas as pl
from jax.experimental.pallas import tpu as pltpu
from jax.sharding import PartitionSpec as P

H = 32
CONV = 4
D = 1024
DI = 2048
CH = 2304
PROJ = 4384
ROWS = 128
SMALL = 16
WIDE = 4480
PACK = WIDE + 2 * D
EPS = 1e-05
PRECISE = lax.Precision.HIGHEST
F32 = jnp.float32
BF16 = jnp.bfloat16
VMEM_LIMIT = 50 * 1024 * 1024


def pass_section(block, distance):
    devices = range(lax.axis_size("section"))
    route = [(i - distance, i) for i in devices if i - distance in devices]
    return lax.ppermute(block, "section", route)


def dot_nt(left, right, precision=None):
    return lax.dot_general(
        left, right, (((1,), (1,)), ((), ())), precision=precision, preferred_element_type=F32
    )


def dot_tn(left, right, precision=None):
    return lax.dot_general(
        left, right, (((0,), (0,)), ((), ())), precision=precision, preferred_element_type=F32
    )


def column_iota(shape, axis):
    return lax.broadcasted_iota(jnp.int32, shape, axis)


def lag_masks(first, filled):
    at = column_iota((ROWS, 1), 0)
    own = (at >= first).astype(jnp.int32) + (at >= filled).astype(jnp.int32)
    masks = []
    for lag in range(1, CONV):
        earlier = (at - lag >= first).astype(jnp.int32) + (at - lag >= filled).astype(jnp.int32)
        masks.append(((at >= lag) & (earlier == own)).astype(F32))
    return masks


def pair_mask(first, filled):
    i = column_iota((ROWS, ROWS), 0)
    j = column_iota((ROWS, ROWS), 1)
    seg_i = (i >= first).astype(jnp.int32) + (i >= filled).astype(jnp.int32)
    seg_j = (j >= first).astype(jnp.int32) + (j >= filled).astype(jnp.int32)
    return (i >= j) & (seg_i == seg_j)


IN_CHUNKS = tuple((start, 512) for start in range(0, 4096, 512)) + ((4096, 384),)


def layer_kernel(
    with_back,
    lens_ref,
    v_ref,
    dout_ref,
    norm_ref,
    taps_ref,
    bias_ref,
    dtb_ref,
    rate_ref,
    skip_ref,
    gate_ref,
    pack_ref,
    *rest,
):
    if with_back:
        (out_ref, outb_ref, dv_ref, dvb_ref, nb_ref, gn_ref, gb_ref, dzx_ref) = rest[:8]
        (dnorm_ref, dtaps_ref, dbias_ref, dgate_ref, dskip_ref, ddtb_ref, drate_ref) = rest[8:15]
        rest = rest[15:]
    else:
        (outb_ref, nb_ref, gn_ref) = rest[:3]
        rest = rest[3:]
    (win, wout, sems, zx, xc, slope, decay, ys, gs, cum_t, dt_t) = rest[:11]
    blocks = win.shape[0]
    quarter = blocks // 4
    block_rows = win.shape[1]

    copies = [
        pltpu.make_async_copy(
            pack_ref.at[:, :, pl.ds(start, size)], win.at[:, :, pl.ds(start, size)], sems.at[k]
        )
        for k, (start, size) in enumerate(IN_CHUNKS)
    ]
    for half in range(2):
        copies.append(
            pltpu.make_async_copy(
                pack_ref.at[:, :, pl.ds(WIDE + half * D, D)],
                wout.at[:, pl.ds(half * block_rows, block_rows), :],
                sems.at[len(IN_CHUNKS) + half],
            )
        )
    for copy in copies:
        copy.start()

    first = lens_ref[0]
    filled = lens_ref[0] + lens_ref[1]
    masks = lag_masks(first, filled)
    active = (column_iota((ROWS, 1), 0) < filled).astype(F32)
    lane = column_iota((ROWS, ROWS), 1)
    low_lanes = lane < 64
    head_lanes = lane < H

    v = v_ref[...].astype(F32)
    r = lax.rsqrt(jnp.mean(v * v, axis=1, keepdims=True) + EPS)
    nb_ref[...] = (v * r * norm_ref[...]).astype(BF16)

    for k, (start, size) in enumerate(IN_CHUNKS):
        copies[k].wait()
        zx[:, pl.ds(start, size)] = jnp.dot(
            nb_ref[...],
            win[:, :, pl.ds(start, size)].reshape(D, size),
            preferred_element_type=F32,
        )

    def conv_step(c, carry):
        at = pl.ds(pl.multiple_of(c * 256, 256), 256)
        u = zx[:, pl.ds(pl.multiple_of(DI + c * 256, 256), 256)]
        taps = taps_ref[:, at]
        total = bias_ref[:, at] + taps[CONV - 1 : CONV] * u
        for lag in range(1, CONV):
            total += taps[CONV - 1 - lag : CONV - lag] * (pltpu.roll(u, lag, 0) * masks[lag - 1])
        sig = jax.nn.sigmoid(total)
        xc[:, at] = total * sig
        if with_back:
            slope[:, at] = sig * (1.0 + total * (1.0 - sig))
        return carry

    lax.fori_loop(0, CH // 256, conv_step, 0)

    raw = jnp.where(head_lanes, zx[:, DI + CH :], 0.0) + dtb_ref[...]
    dt = jnp.maximum(raw, 0.0) + jnp.log1p(jnp.exp(-jnp.abs(raw)))
    dt = jnp.where(head_lanes, dt, 0.0)
    rate = rate_ref[...]
    lower = (column_iota((ROWS, ROWS), 0) >= lane).astype(F32)
    cum = jnp.dot(lower, dt * rate, precision=PRECISE, preferred_element_type=F32)
    cum_t[...] = cum.T
    dt_t[...] = dt.T
    allowed = pair_mask(first, filled)
    bb = xc[:, DI : DI + 128]
    cc = xc[:, DI + 128 :]
    score = dot_nt(cc, bb, PRECISE)

    def head_group(g, carry):
        turned = pltpu.roll(cum, lax.rem(ROWS - 8 * g, ROWS), 1)
        rows = pl.ds(pl.multiple_of(g * 8, 8), 8)
        cum_rows = cum_t[rows, :]
        dt_rows = dt_t[rows, :]
        for pair in range(4):
            at = pl.ds(pl.multiple_of(g * 512 + pair * 128, 128), 128)
            mixes = []
            for k in (2 * pair, 2 * pair + 1):
                gap = turned[:, k : k + 1] - cum_rows[k : k + 1, :]
                fade = jnp.exp(jnp.where(allowed, gap, -1e30))
                if with_back:
                    decay[g * 8 + k] = fade
                mixes.append((score * fade * dt_rows[k : k + 1, :]).astype(BF16))
            x = xc[:, at]
            halves = [jnp.where(low_lanes, x, 0.0), jnp.where(low_lanes, 0.0, x)]
            ys[:, at] = (
                jnp.dot(
                    jnp.concatenate(mixes, axis=1),
                    jnp.concatenate(halves, axis=0).astype(BF16),
                    preferred_element_type=F32,
                )
                + skip_ref[:, at] * x
            )
        return carry

    lax.fori_loop(0, H // 8, head_group, 0)

    def gate_step(c, total):
        at = pl.ds(pl.multiple_of(c * 256, 256), 256)
        z = zx[:, at]
        g = ys[:, at] * (z * jax.nn.sigmoid(z))
        gs[:, at] = g
        return total + jnp.sum(g * g, axis=1, keepdims=True)

    total = lax.fori_loop(0, DI // 256, gate_step, jnp.zeros((ROWS, 1), F32))
    q = lax.rsqrt(total * (1.0 / DI) + EPS)

    def gain_step(c, carry):
        at = pl.ds(pl.multiple_of(c * 256, 256), 256)
        gn_ref[:, at] = (gs[:, at] * q * gate_ref[:, at]).astype(BF16)
        return carry

    lax.fori_loop(0, DI // 256, gain_step, 0)

    for copy in copies[len(IN_CHUNKS) :]:
        copy.wait()

    def branch_step(c, carry):
        at = pl.ds(pl.multiple_of(c * 512, 512), 512)
        branch = jnp.dot(
            gn_ref[...], wout[:, :, at].reshape(DI, 512), preferred_element_type=F32
        )
        result = v_ref[:, at].astype(F32) + active * branch
        outb_ref[:, at] = result.astype(BF16)
        if with_back:
            out_ref[:, at] = result
        return carry

    lax.fori_loop(0, D // 512, branch_step, 0)
    if not with_back:
        return

    (dgs, dxc, row_part, col_part, dscore) = rest[11:]
    gb_ref[...] = (active * dout_ref[...].astype(F32)).astype(BF16)

    def dgate_step(c, total):
        at = pl.ds(pl.multiple_of(c * 512, 512), 512)
        weight = wout[pl.ds(c * quarter, quarter)].reshape(512, D)
        dgn = dot_nt(gb_ref[...], weight)
        g = gs[:, at]
        dgate_ref[:, at] = jnp.sum(dgn * (g * q), axis=0, keepdims=True)
        pulled = dgn * gate_ref[:, at]
        dgs[:, at] = pulled
        return total + jnp.sum(pulled * g, axis=1, keepdims=True)

    total = lax.fori_loop(0, 4, dgate_step, jnp.zeros((ROWS, 1), F32))
    pull = q * q * q * (total * (1.0 / DI))

    def dz_step(c, carry):
        at = pl.ds(pl.multiple_of(c * 256, 256), 256)
        dg = q * dgs[:, at] - gs[:, at] * pull
        z = zx[:, at]
        sig = jax.nn.sigmoid(z)
        dy = dg * (z * sig)
        dgs[:, at] = dy
        dzx_ref[:, at] = (dg * ys[:, at] * (sig * (1.0 + z * (1.0 - sig)))).astype(BF16)
        dskip_ref[:, at] = jnp.sum(dy * xc[:, at], axis=0, keepdims=True)
        return carry

    lax.fori_loop(0, DI // 256, dz_step, 0)

    row_part[...] = jnp.zeros((ROWS, ROWS), F32)
    col_part[...] = jnp.zeros((ROWS, ROWS), F32)
    dscore[...] = jnp.zeros((ROWS, ROWS), F32)

    def head_back(g, carry):
        rows = pl.ds(pl.multiple_of(g * 8, 8), 8)
        dt_rows = dt_t[rows, :]
        col_sums = []
        row_sum = row_part[...]
        dscore_sum = dscore[...]
        for pair in range(4):
            at = pl.ds(pl.multiple_of(g * 512 + pair * 128, 128), 128)
            dy = dgs[:, at]
            dys = jnp.concatenate(
                [jnp.where(low_lanes, dy, 0.0), jnp.where(low_lanes, 0.0, dy)], axis=0
            ).astype(BF16)
            dmix = dot_nt(dys, xc[:, at].astype(BF16))
            mixes = []
            for side in range(2):
                k = 2 * pair + side
                dt_row = dt_rows[k : k + 1, :]
                fade = decay[g * 8 + k]
                part = dmix[side * ROWS : (side + 1) * ROWS] * fade
                dscore_sum += part * dt_row
                part = part * score
                col_sums.append(jnp.sum(part, axis=0, keepdims=True))
                row_sum += jnp.where(
                    lane == g * 8 + k, jnp.sum(part * dt_row, axis=1, keepdims=True), 0.0
                )
                mixes.append((score * fade * dt_row).astype(BF16))
            dxc[:, at] = dot_tn(jnp.concatenate(mixes, axis=0), dys) + skip_ref[:, at] * dy
        col_part[rows, :] = jnp.concatenate(col_sums, axis=0)
        row_part[...] = row_sum
        dscore[...] = dscore_sum
        return carry

    lax.fori_loop(0, H // 8, head_back, 0)

    col_sum = col_part[...].T
    dcum = row_part[...] - dt * col_sum
    dlog = dot_tn(lower, dcum, PRECISE)
    drate_ref[...] = jnp.sum(dlog * dt, axis=0, keepdims=True) * rate
    draw = jnp.where(head_lanes, (col_sum + dlog * rate) * jax.nn.sigmoid(raw), 0.0)
    ddtb_ref[...] = jnp.sum(draw, axis=0, keepdims=True)
    dzx_ref[:, DI + CH :] = draw.astype(BF16)
    dxc[:, DI : DI + 128] = dot_tn(dscore[...], cc, PRECISE)
    dxc[:, DI + 128 :] = jnp.dot(dscore[...], bb, precision=PRECISE, preferred_element_type=F32)

    def dconv_step(c, carry):
        at = pl.ds(pl.multiple_of(c * 256, 256), 256)
        wide_at = pl.ds(pl.multiple_of(DI + c * 256, 256), 256)
        u = zx[:, wide_at]
        taps = taps_ref[:, at]
        dconv = dxc[:, at] * slope[:, at]
        dbias_ref[:, at] = jnp.sum(dconv, axis=0, keepdims=True)
        du = taps[CONV - 1 : CONV] * dconv
        dtaps_ref[CONV - 1 : CONV, at] = jnp.sum(dconv * u, axis=0, keepdims=True)
        for lag in range(1, CONV):
            masked = dconv * masks[lag - 1]
            k = CONV - 1 - lag
            dtaps_ref[k : k + 1, at] = jnp.sum(
                masked * pltpu.roll(u, lag, 0), axis=0, keepdims=True
            )
            du += taps[k : k + 1] * pltpu.roll(masked, ROWS - lag, 0)
        dzx_ref[:, wide_at] = du.astype(BF16)
        return carry

    lax.fori_loop(0, CH // 256, dconv_step, 0)

    def dnorm_step(c, total):
        at = pl.ds(pl.multiple_of(c * 256, 256), 256)
        weight = win[pl.ds(c * quarter, quarter)].reshape(256, WIDE)
        dnormed = dot_nt(dzx_ref[...], weight)
        vc = v_ref[:, at].astype(F32)
        dnorm_ref[:, at] = jnp.sum(dnormed * (vc * r), axis=0, keepdims=True)
        pulled = dnormed * norm_ref[:, at]
        dv_ref[:, at] = pulled
        return total + jnp.sum(pulled * vc, axis=1, keepdims=True)

    total = lax.fori_loop(0, 4, dnorm_step, jnp.zeros((ROWS, 1), F32))
    pull = r * r * r * (total * (1.0 / D))

    def dv_step(c, carry):
        at = pl.ds(pl.multiple_of(c * 256, 256), 256)
        result = (
            dout_ref[:, at].astype(F32) + r * dv_ref[:, at] - v_ref[:, at].astype(F32) * pull
        )
        dv_ref[:, at] = result
        dvb_ref[:, at] = result.astype(BF16)
        return carry

    lax.fori_loop(0, D // 256, dv_step, 0)


def run_layer(with_back, lens, v, dout, params, pack):
    blocks, block_rows = pack.shape[0], pack.shape[1]
    vmem = pl.BlockSpec(memory_space=pltpu.VMEM)
    shape = jax.ShapeDtypeStruct
    if with_back:
        outs = [
            shape((ROWS, D), F32),
            shape((ROWS, D), BF16),
            shape((ROWS, D), F32),
            shape((ROWS, D), BF16),
            shape((ROWS, D), BF16),
            shape((ROWS, DI), BF16),
            shape((ROWS, D), BF16),
            shape((ROWS, WIDE), BF16),
            shape((1, D), F32),
            shape((CONV, CH), F32),
            shape((1, CH), F32),
            shape((1, DI), F32),
            shape((1, DI), F32),
            shape((1, ROWS), F32),
            shape((1, ROWS), F32),
        ]
    else:
        outs = [shape((ROWS, D), BF16), shape((ROWS, D), BF16), shape((ROWS, DI), BF16)]
    scratch = [
        pltpu.VMEM((blocks, block_rows, WIDE), BF16),
        pltpu.VMEM((blocks, 2 * block_rows, D), BF16),
        pltpu.SemaphoreType.DMA((len(IN_CHUNKS) + 2,)),
        pltpu.VMEM((ROWS, WIDE), F32),
        pltpu.VMEM((ROWS, CH), F32),
        pltpu.VMEM((ROWS, CH), F32),
        pltpu.VMEM((H, ROWS, ROWS), F32),
        pltpu.VMEM((ROWS, DI), F32),
        pltpu.VMEM((ROWS, DI), F32),
        pltpu.VMEM((ROWS, ROWS), F32),
        pltpu.VMEM((ROWS, ROWS), F32),
    ]
    if with_back:
        scratch += [
            pltpu.VMEM((ROWS, DI), F32),
            pltpu.VMEM((ROWS, CH), F32),
            pltpu.VMEM((ROWS, ROWS), F32),
            pltpu.VMEM((ROWS, ROWS), F32),
            pltpu.VMEM((ROWS, ROWS), F32),
        ]
    flops = 2 * ROWS * (WIDE * D + DI * D) * (2 if with_back else 1)
    return pl.pallas_call(
        functools.partial(layer_kernel, with_back),
        out_shape=outs,
        in_specs=[pl.BlockSpec(memory_space=pltpu.SMEM)]
        + [vmem] * 9
        + [pl.BlockSpec(memory_space=pl.ANY)],
        out_specs=[vmem] * len(outs),
        scratch_shapes=scratch,
        cost_estimate=pl.CostEstimate(
            flops=flops, bytes_accessed=D * PACK * 2, transcendentals=H * ROWS * ROWS
        ),
        compiler_params=pltpu.CompilerParams(vmem_limit_bytes=VMEM_LIMIT),
        name="layer_both" if with_back else "layer_forward",
    )(lens, v, dout, *params, pack)


GRAD_CHUNK = 640


def in_grad_kernel(first_ref, second_ref, dzx_ref, dzx2_ref, extra_ref, out_ref, turned):
    step = pl.program_id(0)

    @pl.when(step == 0)
    def _():
        turned[:, :ROWS] = first_ref[...].T
        turned[:, ROWS:] = second_ref[...].T

    both = jnp.concatenate([dzx_ref[...], dzx2_ref[...]], axis=0)
    grad = jnp.dot(turned[...], both, preferred_element_type=F32).astype(BF16)
    out_ref[...] = grad.reshape(out_ref.shape)

    @pl.when(step == WIDE // GRAD_CHUNK - 1)
    def _():
        last = pl.ds(GRAD_CHUNK - 128, 128)
        spare = lax.broadcasted_iota(jnp.int32, extra_ref.shape, 2) >= PROJ - WIDE + 128
        kept = out_ref[:, :, last].astype(F32)
        out_ref[:, :, last] = jnp.where(spare, extra_ref[...].astype(F32), kept).astype(BF16)


def in_grad(first, second, dzx, dzx2, extra):
    blocks, block_rows = extra.shape[0], extra.shape[1]
    return pl.pallas_call(
        in_grad_kernel,
        grid=(WIDE // GRAD_CHUNK,),
        out_shape=jax.ShapeDtypeStruct((blocks, block_rows, WIDE), BF16),
        in_specs=[
            pl.BlockSpec((ROWS, D), lambda i: (0, 0)),
            pl.BlockSpec((ROWS, D), lambda i: (0, 0)),
            pl.BlockSpec((ROWS, GRAD_CHUNK), lambda i: (0, i)),
            pl.BlockSpec((ROWS, GRAD_CHUNK), lambda i: (0, i)),
            pl.BlockSpec((blocks, block_rows, 128), lambda i: (0, 0, 0)),
        ],
        out_specs=pl.BlockSpec((blocks, block_rows, GRAD_CHUNK), lambda i: (0, 0, i)),
        scratch_shapes=[pltpu.VMEM((D, 2 * ROWS), BF16)],
        cost_estimate=pl.CostEstimate(
            flops=4 * ROWS * D * WIDE, bytes_accessed=D * WIDE * 2, transcendentals=0
        ),
        compiler_params=pltpu.CompilerParams(vmem_limit_bytes=VMEM_LIMIT),
        name="in_weight_grad",
    )(first, second, dzx, dzx2, extra)


def small_cuts(n):
    cuts = [0]
    for size in (D, CONV * CH, CH, DI):
        cuts.append(cuts[-1] + size // n)
    return list(zip(cuts[:-1], cuts[1:]))


def gather_weights(in_shard, out_shard, norm, conv, bias, gate):
    rows = in_shard.shape[0]
    n = lax.axis_size("dp")
    small = jnp.concatenate([norm, conv.reshape(-1), bias, gate])
    small = jnp.pad(small, (0, rows * SMALL - small.shape[0])).reshape(rows, SMALL)
    zeros = jnp.zeros((rows, WIDE - PROJ - SMALL), BF16)
    pack = jnp.concatenate([in_shard, small, zeros, out_shard[:rows], out_shard[rows:]], axis=1)
    whole = lax.all_gather(pack, "dp", axis=0, tiled=False)
    flat = whole[:, :, PROJ : PROJ + SMALL].reshape(n, rows * SMALL).astype(F32)
    norm_all, conv_all, bias_all, gate_all = [flat[:, a:b] for a, b in small_cuts(n)]
    conv_all = conv_all.reshape(n, CONV, CH // n).transpose(1, 0, 2).reshape(CONV, CH)
    return (whole, norm_all.reshape(1, D), conv_all, bias_all.reshape(1, CH), gate_all.reshape(1, DI))


def high_low(values):
    high = values.astype(BF16)
    return high, (values - high.astype(F32)).astype(BF16)


def pack_small(norm, conv, bias, gate, heads, n, rows):
    conv_rows = conv.reshape(CONV, n, CH // n).transpose(1, 0, 2).reshape(n, -1)
    small = jnp.concatenate(
        [norm.reshape(n, -1), conv_rows, bias.reshape(n, -1), gate.reshape(n, -1)], axis=1
    )
    small = jnp.pad(small, ((0, 0), (0, rows * SMALL - small.shape[1])))
    heads = jnp.broadcast_to(heads[None], (n, heads.shape[0]))
    heads = jnp.pad(heads, ((0, 0), (0, rows * SMALL - heads.shape[1])))
    extra = [item.reshape(n, rows, SMALL) for item in (*high_low(small), *high_low(heads))]
    before = jnp.zeros((n, rows, PROJ - WIDE + 128), BF16)
    after = jnp.zeros((n, rows, WIDE - PROJ - 4 * SMALL), BF16)
    return jnp.concatenate([before, *extra, after], axis=2)


def body(
    inputs,
    cotangent,
    seq_lengths,
    norm_gain,
    in_weight,
    conv_weight,
    conv_bias,
    dt_bias,
    a_log,
    skip_gain,
    gate_gain,
    out_weight,
):
    section = lax.axis_index("section")
    is_first = section == 0
    n = lax.axis_size("dp")
    rows = in_weight.shape[1]
    pack, norm_all, conv_all, bias_all, gate_all = gather_weights(
        in_weight[0], out_weight[0], norm_gain[0], conv_weight[0], conv_bias[0], gate_gain[0]
    )
    spare = ROWS - H
    params = (
        norm_all,
        conv_all,
        bias_all,
        jnp.pad(dt_bias.astype(F32), ((0, 0), (0, spare))),
        jnp.pad(-jnp.exp(a_log.astype(F32)), ((0, 0), (0, spare))),
        jnp.repeat(skip_gain.astype(F32), DI // H, axis=1),
        gate_all,
    )

    def pick(first, second):
        return jnp.where(is_first, first, second)

    out1, _, _ = run_layer(False, seq_lengths[0], inputs[0], cotangent[0], params, pack)
    lens2 = pick(seq_lengths[1], seq_lengths[0])
    came = pass_section(out1, 1)
    two = run_layer(True, lens2, pick(inputs[1], came), cotangent[0], params, pack)
    lens3 = pick(seq_lengths[0], seq_lengths[1])
    came = pass_section(two[1], 1)
    pulled = pass_section(two[3], -1)
    three = run_layer(
        True, lens3, pick(inputs[0], came), pick(pulled, cotangent[1]), params, pack
    )
    pulled = pass_section(three[3], -1)
    four = run_layer(True, seq_lengths[1], inputs[1], pulled, params, pack)

    section_outputs = jnp.stack(
        [pick(three[1].astype(F32), two[0]), pick(two[1].astype(F32), three[0])]
    )
    input_grads = jnp.stack(
        [pick(three[2], two[3].astype(F32)), pick(four[2], three[3].astype(F32))]
    )

    active = jnp.arange(ROWS)[:, None] < jnp.sum(seq_lengths[1])
    branch_grad = pick(jnp.where(active, pulled, jnp.zeros_like(pulled)), two[6])
    grad_out = jnp.einsum(
        "tf,td->fd",
        jnp.concatenate([two[5], three[5]]),
        jnp.concatenate([branch_grad, three[6]]),
        preferred_element_type=F32,
    ).astype(BF16)
    got_out = lax.all_to_all(grad_out.reshape(n, 2 * rows, D), "dp", 0, 0)

    smalls = [pick(four[i], two[i]) + three[i] for i in range(8, 15)]
    norm_s, conv_s, bias_s, gate_s, skip_s, dtb_s, rate_s = smalls
    heads = jnp.concatenate(
        [dtb_s[0, :H], rate_s[0, :H], jnp.sum(skip_s.reshape(H, DI // H), axis=1)]
    )
    extra = pack_small(norm_s, conv_s, bias_s, gate_s, heads, n, rows)
    grad_in = in_grad(two[4], three[4], pick(four[7], two[7]), three[7], extra)
    got_in = lax.all_to_all(grad_in, "dp", 0, 0)
    sum_out = jnp.sum(got_out.astype(F32), axis=0)
    sum_in = jnp.sum(got_in.astype(F32), axis=0)
    own = [sum_in[:, PROJ + i * SMALL : PROJ + (i + 1) * SMALL].reshape(-1) for i in range(4)]
    flat, heads = own[0] + own[1], own[2] + own[3]
    norm_g, conv_g, bias_g, gate_g = [flat[a:b] for a, b in small_cuts(n)]
    return (
        section_outputs[None],
        input_grads[None],
        norm_g[None],
        sum_in[None, :, :PROJ],
        conv_g.reshape(1, CONV, -1),
        bias_g[None],
        heads[None, :H],
        heads[None, H : 2 * H],
        heads[None, 2 * H : 3 * H],
        gate_g[None],
        sum_out[None],
    )


def solution(mesh):
    in_specs = (
        P(None, "dp", None),
        P(None, "dp", None),
        P(None, "dp"),
        P("section", "dp"),
        P("section", "dp", None),
        P("section", None, "dp"),
        P("section", "dp"),
        P("section", None),
        P("section", None),
        P("section", None),
        P("section", "dp"),
        P("section", "dp", None),
    )
    out_specs = (
        P("section", None, "dp", None),
        P("section", None, "dp", None),
        P("section", "dp"),
        P("section", "dp", None),
        P("section", None, "dp"),
        P("section", "dp"),
        P("section", None),
        P("section", None),
        P("section", None),
        P("section", "dp"),
        P("section", "dp", None),
    )
    return jax.shard_map(body, mesh=mesh, in_specs=in_specs, out_specs=out_specs, check_vma=False)
```

time: 1600 us -> 414 us (0.26)
  the two profiles are of different devices: /device:TPU:0 before, /device:TPU:22 now
where the time goes in v2:
time: 414 us; the launch traced here: 413 us
  waiting for transfers between devices  233 us (56%)
  Pallas kernels  84.1 us (20%)
  starting transfers between devices  33.1 us (8%)
  local copies, waits for them, and re-layouts  23.3 us (6%)
  other arithmetic  21.1 us (5%)
  between operations  14.5 us (4%)
    all_to_all x1, waiting for transfers between devices, body(): got_in = lax.all_to_all(grad_in, 'dp', 0, 0)  133 us
    all_gather x1, waiting for transfers between devices, gather_weights(): whole = lax.all_gather(pack, 'dp', axis=0, tiled=False)  90.4 us
    pallas_call x4, Pallas kernels, run_layer(): pl.pallas_call(functools.partial(layer_kernel, with_back), out_shape=outs...  76.7 us
    all_to_all x1, starting transfers between devices, body(): got_in = lax.all_to_all(grad_in, 'dp', 0, 0)  17.1 us
    all_to_all x1, starting transfers between devices, body(): got_out = lax.all_to_all(grad_out.reshape(n, 2 * rows, D), 'dp', 0, 0)  9.12 us
  transfers between devices with their start and end apart: 7, of which 6 were waited for; matrix products, arithmetic and copies ran while one was open for 6% of the time, Pallas kernels for 7%

profile of v2, /device:TPU:22, one launch (start us, length us, event | category | flops | bytes accessed | tf_op | source)
XLA Modules:
  0.0 412.7 jit_solution(2015089290680627850)
XLA Ops:
  7.2 0.8 reshape_squeeze.3
  8.0 0.8 fusion.23
  8.8 0.8 slice_bitcast_fusion.4
  9.6 1.7 concatenate.22
  11.3 0.7 bitcast_convert_fusion
  12.1 0.7 exponential_negate_fusion
  12.8 0.7 pad_convert_fusion.dtb_ref
  13.5 1.4 slice_reduce_fusion
  14.9 1.0 slice_bitcast_fusion.1.dout_ref
  15.8 1.1 slice_bitcast_fusion.2
  16.9 90.4 %all-gather.3.cloned.1.call-done = bf16[1024,6528]{1,0:T(8,128)(2,1)} async-done(((bf16[16,6528]{1,0:T(8,128)(2,1)}), bf16[1024,6528]{1,0:T(8,128)(2,1)}) %all-gather.3.cloned.1.call-update) | async-done | bytes 13369360 | tf_op jit(solution)/shard_map/all_gather | solution.py:470
  107.3 1.1 slice_convert_fusion
  108.4 0.3 copy.36
  108.9 0.1 copy.38
  109.0 0.1 reshape.122.taps_ref
  109.2 0.1 reshape.123.bias_ref
  109.5 10.3 %layer_forward.1 = (bf16[128,1024]{1,0:T(8,128)(2,1)S(1)}, bf16[128,1024]{1,0:T(8,128)(2,1)}, bf16[128,2048]{1,0:T(8,128)(2,1)}) custom-call(s32[2]{0:T(128)S(1)} %get-tuple-element.102.lens_ref, bf16[128,1024]{1,0:T(8,128)(2,1)S(1)} %get-tuple-element.92.v_ref, bf16[128,1024]{1,0:T(8,128)(2,1)S(1)} %slice_bitcast_fusion.1.dout_ref, ...), custom_call_target="tpu_custom_call" | custom-call | flops 1711276032 | bytes 13369344 | tf_op jit(solution)/shard_map/layer_forward/pallas_call | solution.py:394
  119.8 1.7 collective-permute-start
  121.6 1.1 collective-permute-done
  122.7 22.0 %layer_both.3 = (f32[128,1024]{1,0:T(8,128)S(1)}, bf16[128,1024]{1,0:T(8,128)(2,1)S(1)}, f32[128,1024]{1,0:T(8,128)}, bf16[128,1024]{1,0:T(8,128)(2,1)S(1)}, bf1...) custom-call(s32[2]{0:T(128)S(1)} %get-tuple-element.103.lens_ref, ...), custom_call_target="tpu_custom_call" | custom-call | flops 3422552064 | bytes 13369344 | tf_op jit(solution)/shard_map/layer_both/pallas_call | solution.py:394
  144.8 2.3 collective-permute-start.1
  147.1 1.5 collective-permute-start.2
  148.6 1.9 collective-permute-done.2
  150.6 21.8 %layer_both.4 = (f32[128,1024]{1,0:T(8,128)S(1)}, bf16[128,1024]{1,0:T(8,128)(2,1)S(1)}, f32[128,1024]{1,0:T(8,128)S(1)}, bf16[128,1024]{1,0:T(8,128)(2,1)S(1)},...) custom-call(s32[2]{0:T(128)S(1)} %get-tuple-element.104.lens_ref, ...), custom_call_target="tpu_custom_call" | custom-call | flops 3422552064 | bytes 13369344 | tf_op jit(solution)/shard_map/layer_both/pallas_call | solution.py:394
  172.4 1.3 collective-permute-start.3
  173.7 0.7 iota_compare_fusion.2
  174.4 1.5 collective-permute-done.3.dout_ref
  176.0 3.2 convolution_convert_fusion
  179.2 9.1 %all-to-all-start.1 = ((bf16[64,32,1024]{2,1,0:T(8,128)(2,1)}), bf16[64,32,1024]{2,1,0:T(8,128)(2,1)}, u32[]{:S(2)}, u32[]{:S(2)}) async-start(bf16[64,32,1024]{2,1,0:T(8,128)(2,1)} %bitcast.74), calls=%async_computation.1 | async-start | bytes 8388608 | tf_op jit(solution)/shard_map/all_to_all | solution.py:559
  188.4 22.6 %layer_both.5 = (f32[128,1024]{1,0:T(8,128)}, bf16[128,1024]{1,0:T(8,128)(2,1)}, f32[128,1024]{1,0:T(8,128)S(1)}, bf16[128,1024]{1,0:T(8,128)(2,1)}, bf16[128,10...) custom-call(s32[2]{0:T(128)S(1)} %get-tuple-element.101.lens_ref, ...), custom_call_target="tpu_custom_call" | custom-call | flops 3422552064 | bytes 13369344 | tf_op jit(solution)/shard_map/layer_both/pallas_call | solution.py:394
  211.1 0.7 copy.44
  212.0 0.6 select_add_fusion
  212.6 0.9 reshape.126
  213.6 0.7 copy.41
  214.3 0.9 reshape.127
  215.4 0.7 fusion.6
  216.1 0.9 copy.45
  217.1 0.7 subtract_convert_fusion
  217.8 0.9 copy.46
  218.8 0.1 reduce_sum.36
  219.2 0.8 pad.34
  220.0 0.7 pad.35
  220.7 0.7 broadcast.33
  221.4 1.8 concatenate.25.extra_ref
  223.3 1.4 broadcast_select_fusion.dzx_ref
  224.7 0.9 copy-done.2
  225.6 0.9 copy-done.8
  226.6 7.4 %in_weight_grad.1 = bf16[64,16,4480]{2,1,0:T(8,128)(2,1)} custom-call(bf16[128,1024]{1,0:T(8,128)(2,1)S(1)} %copy-done.2, bf16[128,1024]{1,0:T(8,128)(2,1)S(1)} %copy-done.8, bf16[128,4480]{1,0:T(8,128)(2,1)S(1)} %broadcast_select_fusion.dzx_ref, bf16[128,4480]{1,0:T(8,128)(2,1)S(1)} %copy-done, bf16[64,16,128]{2,1,0:T(8,128)(2,1)S(1)} %concatenate.25.extra_ref), custom_call_target="tpu_custom_call" | custom-call | flops 2348810240 | bytes 9175040 | tf_op jit(solution)/shard_map/in_weight_grad/pallas_call | solution.py:435
  234.0 5.3 %all-to-all-done.1 = bf16[64,32,1024]{2,1,0:T(8,128)(2,1)} async-done(((bf16[64,32,1024]{2,1,0:T(8,128)(2,1)}), bf16[64,32,1024]{2,1,0:T(8,128)(2,1)}, u32[]{:S(2)}, u32[]{:S(2)}) %all-to-all-start.1) | async-done | bytes 4194336 | tf_op jit(solution)/shard_map/all_to_all | solution.py:559
  239.3 17.1 %all-to-all-start = ((bf16[64,16,4480]{2,1,0:T(8,128)(2,1)}), bf16[64,16,4480]{2,1,0:T(8,128)(2,1)}, u32[]{:S(2)}, u32[]{:S(2)}) async-start(bf16[64,16,4480]{2,1,0:T(8,128)(2,1)} %in_weight_grad.1), calls=%async_computation | async-start | bytes 18350080 | tf_op jit(solution)/shard_map/all_to_all | solution.py:568
  256.5 0.2 select_bitcast_fusion.1
  256.7 1.0 maximum_bitcast_fusion
  257.8 1.1 maximum_bitcast_fusion.1
  258.9 3.7 convert_reduce_fusion.1
  262.6 133.2 %all-to-all-done = bf16[64,16,4480]{2,1,0:T(8,128)(2,1)} async-done(((bf16[64,16,4480]{2,1,0:T(8,128)(2,1)}), bf16[64,16,4480]{2,1,0:T(8,128)(2,1)}, u32[]{:S(2)}, u32[]{:S(2)}) %all-to-all-start) | async-done | bytes 9175072 | tf_op jit(solution)/shard_map/all_to_all | solution.py:568
  395.8 5.1 %convert_reduce_fusion = f32[16,4480]{1,0:T(8,128)S(1)} fusion(bf16[64,16,4480]{2,1,0:T(8,128)(2,1)} %all-to-all-done), kind=kLoop, calls=%fused_computation | loop fusion | flops 9103360 | bytes 9461760 | tf_op jit(solution)/shard_map/reduce_sum | solution.py:570
  400.9 0.7 slice_bitcast_fusion
  401.7 0.5 slice.136
  402.3 0.6 slice_bitcast_fusion.7
  402.8 0.6 slice_bitcast_fusion.6
  403.4 0.7 reshape.133
  404.1 0.6 broadcast_in_dim.59
  404.7 0.6 broadcast_in_dim.60
  405.3 0.6 broadcast_in_dim.61
  (76 shorter events, 2.1 us)
Async XLA Ops:
  7.2 100.1 %all-gather.3.cloned.1.call-start = ((), (), s32[]{:S(2)}) async-start(), calls=%async_computation.2 | async-start | bytes 13578240 | tf_op jit(solution)/shard_map/all_gather | solution.py:470
  109.5 12.1 %copy-start.16 = (s32[2,2]{1,0:T(2,128)S(1)}, s32[2,2]{1,0:T(2,128)}, u32[]{:S(2)}) copy-start(s32[2,2]{1,0:T(2,128)} %param.14) | copy-start | bytes 52
  109.5 13.2 %copy-start.13 = (bf16[2,128,1024]{2,1,0:T(8,128)(2,1)S(1)}, bf16[2,128,1024]{2,1,0:T(8,128)(2,1)}, u32[]{:S(2)}) copy-start(bf16[2,128,1024]{2,1,0:T(8,128)(2,1)} %param.12) | copy-start | bytes 1572868
  119.8 2.9 collective-permute-start
  122.7 25.9 %copy-start.14 = (bf16[2,128,1024]{2,1,0:T(8,128)(2,1)S(1)}, bf16[2,128,1024]{2,1,0:T(8,128)(2,1)}, u32[]{:S(2)}) copy-start(bf16[2,128,1024]{2,1,0:T(8,128)(2,1)} %param.12) | copy-start | bytes 1572868
  122.7 27.8 %copy-start.15 = (bf16[2,128,1024]{2,1,0:T(8,128)(2,1)S(1)}, bf16[2,128,1024]{2,1,0:T(8,128)(2,1)}, u32[]{:S(2)}) copy-start(bf16[2,128,1024]{2,1,0:T(8,128)(2,1)} %param.13) | copy-start | bytes 1572868
  144.8 3.9 copy-start.9
  144.8 5.8 %copy-start.1 = (bf16[128,1024]{1,0:T(8,128)(2,1)}, bf16[128,1024]{1,0:T(8,128)(2,1)S(1)}, u32[]{:S(2)}) copy-start(bf16[128,1024]{1,0:T(8,128)(2,1)S(1)} %get-tuple-element.59.first_ref) | copy-start | bytes 786436
  144.8 27.6 %copy-start.11 = (bf16[128,1024]{1,0:T(8,128)(2,1)}, bf16[128,1024]{1,0:T(8,128)(2,1)S(1)}, u32[]{:S(2)}) copy-start(bf16[128,1024]{1,0:T(8,128)(2,1)S(1)} %get-tuple-element.52) | copy-start | bytes 786436
  144.8 3.8 collective-permute-start.1
  147.1 3.4 collective-permute-start.2
  172.4 6.8 %copy-start.3 = (bf16[128,1024]{1,0:T(8,128)(2,1)}, bf16[128,1024]{1,0:T(8,128)(2,1)S(1)}, u32[]{:S(2)}) copy-start(bf16[128,1024]{1,0:T(8,128)(2,1)S(1)} %get-tuple-element.57) | copy-start | bytes 786436
  172.4 6.8 %copy-start.5 = (bf16[128,1024]{1,0:T(8,128)(2,1)}, bf16[128,1024]{1,0:T(8,128)(2,1)S(1)}, u32[]{:S(2)}) copy-start(bf16[128,1024]{1,0:T(8,128)(2,1)S(1)} %get-tuple-element.53) | copy-start | bytes 786436
  172.4 6.8 %copy-start.7 = (bf16[128,1024]{1,0:T(8,128)(2,1)}, bf16[128,1024]{1,0:T(8,128)(2,1)S(1)}, u32[]{:S(2)}) copy-start(bf16[128,1024]{1,0:T(8,128)(2,1)S(1)} %get-tuple-element.60.second_ref) | copy-start | bytes 786436
  172.4 3.4 collective-permute-start.3
  179.2 60.1 %all-to-all-start.1 = ((bf16[64,32,1024]{2,1,0:T(8,128)(2,1)}), bf16[64,32,1024]{2,1,0:T(8,128)(2,1)}, u32[]{:S(2)}, u32[]{:S(2)}) async-start(bf16[64,32,1024]{2,1,0:T(8,128)(2,1)} %bitcast.74), calls=%async_computation.1 | async-start | bytes 8388608 | tf_op jit(solution)/shard_map/all_to_all | solution.py:559
  210.9 13.7 %copy-start = (bf16[128,4480]{1,0:T(8,128)(2,1)S(1)}, bf16[128,4480]{1,0:T(8,128)(2,1)}, u32[]{:S(2)}) copy-start(bf16[128,4480]{1,0:T(8,128)(2,1)} %get-tuple-element.63.dzx2_ref) | copy-start | bytes 3440644
  224.7 1.0 copy-start.2
  225.6 0.9 copy-start.8
  234.0 22.5 %copy-start.6 = (bf16[128,1024]{1,0:T(8,128)(2,1)S(1)}, bf16[128,1024]{1,0:T(8,128)(2,1)}, u32[]{:S(2)}) copy-start(bf16[128,1024]{1,0:T(8,128)(2,1)} %copy-done.5) | copy-start | bytes 786436
  234.0 22.5 %copy-start.10 = (bf16[128,1024]{1,0:T(8,128)(2,1)S(1)}, bf16[128,1024]{1,0:T(8,128)(2,1)}, u32[]{:S(2)}) copy-start(bf16[128,1024]{1,0:T(8,128)(2,1)} %copy-done.9) | copy-start | bytes 786436
  234.0 22.6 %copy-start.12 = (bf16[128,1024]{1,0:T(8,128)(2,1)S(1)}, bf16[128,1024]{1,0:T(8,128)(2,1)}, u32[]{:S(2)}) copy-start(bf16[128,1024]{1,0:T(8,128)(2,1)} %copy-done.11) | copy-start | bytes 786436
  239.3 156.5 %all-to-all-start = ((bf16[64,16,4480]{2,1,0:T(8,128)(2,1)}), bf16[64,16,4480]{2,1,0:T(8,128)(2,1)}, u32[]{:S(2)}, u32[]{:S(2)}) async-start(bf16[64,16,4480]{2,1,0:T(8,128)(2,1)} %in_weight_grad.1), calls=%async_computation | async-start | bytes 18350080 | tf_op jit(solution)/shard_map/all_to_all | solution.py:568
  256.4 1.3 copy-start.4
Sparse Core Ops, SparseCore 0:
  11.4 95.8 all-gather.2
